TPU v7x, 32 devices: a whole 2x2x4 slice. The times are simulated.
32 devices in a mesh: dp: 32 (over z, y, x, core).
Axes of the slice: x: 2, y: 2, z: 4, core: 2. Of those that a mesh axis runs over, the one named last changes fastest.
Arguments:
- fields: bfloat16 [32, 4, 1024, 384], P('dp'), may hold values from -6 to 6
- conditions: bfloat16 [32, 4, 384], P('dp'), may hold values from -6 to 6
- step_counts: int32 [32], P('dp'), may hold values from 1 to 4, as said below
- cotangent: bfloat16 [32, 4, 1024, 384], P('dp'), may hold values from -6 to 6
- w_ada: bfloat16 [384, 2304], P('dp'), may hold values from -0.15625 to 0.15625
- b_ada: bfloat16 [2304], P('dp'), may hold values from -3 to 3
- w_qkv: bfloat16 [384, 1152], P('dp'), may hold values from -0.3125 to 0.3125
- w_out: bfloat16 [384, 384], P('dp'), may hold values from -1.25 to 1.25
- b_out: bfloat16 [384], P('dp'), may hold values from -2 to 2
- w_up: bfloat16 [384, 1536], P('dp'), may hold values from -0.3125 to 0.3125
- b_up: bfloat16 [1536], P('dp'), may hold values from -3 to 3
- w_down: bfloat16 [1536, 384], P('dp'), may hold values from -0.15625 to 0.15625
- b_down: bfloat16 [384], P('dp'), may hold values from -2 to 2
Outputs:
- layer_output: bfloat16 [32, 4, 1024, 384], P('dp')
- field_grad: float32 [32, 4, 1024, 384], P('dp')
- grad_w_ada: float32 [384, 2304], P('dp')
- grad_b_ada: float32 [2304], P('dp')
- grad_w_qkv: float32 [384, 1152], P('dp')
- grad_w_out: float32 [384, 384], P('dp')
- grad_b_out: float32 [384], P('dp')
- grad_w_up: float32 [384, 1536], P('dp')
- grad_b_up: float32 [1536], P('dp')
- grad_w_down: float32 [1536, 384], P('dp')
- grad_b_down: float32 [384], P('dp')
Inputs may be any that keep to these rules, and one draw needn't show every extreme that they name: `step_counts`: each item has at least one step; some item has 4 steps and some item has one.
All inputs are finite; a program needn't handle non-finite values.
Results may differ from a plain program's by a relative error of at most 0.02.
Values may be sent and summed in bfloat16 or wider, within the bound.
No kernel may reach another device: no remote copies, remote signals or barrier semaphores. Data moves between devices by JAX's collectives and lax.ppermute only.
A program may use at most 192 MiB of HBM per device.

v0:
```python
import functools
import math

import jax
import jax.numpy as jnp
from jax import lax
from jax.experimental import pallas as pl
from jax.experimental.pallas import tpu as pltpu
from jax.sharding import PartitionSpec as P

HEAD = 64
PAIR = 2 * HEAD
EPS = 1e-6
LOG2E = 1.4426950408889634
VMEM_LIMIT = 60 * 2**20
bf16 = jnp.bfloat16
f32 = jnp.float32
shape_of = jax.ShapeDtypeStruct


def dot(left, right, left_dim=1, right_dim=0):
    return lax.dot_general(
        left, right, (((left_dim,), (right_dim,)), ((), ())), preferred_element_type=f32
    )


def norm(value):
    mean = jnp.mean(value, -1, keepdims=True)
    cent = value - mean
    var = jnp.mean(cent * cent, -1, keepdims=True)
    rstd = lax.rsqrt(var + EPS)
    return cent * rstd, rstd


def row_sum(value):
    return jnp.sum(value, 0, keepdims=True)


def up_to(value, unit):
    return -(-value // unit) * unit


def call(body, grid, in_specs, out_specs, out_shape, scratch, name, flops, args):
    return pl.pallas_call(
        body,
        grid_spec=pltpu.PrefetchScalarGridSpec(
            num_scalar_prefetch=1,
            grid=grid,
            in_specs=in_specs,
            out_specs=out_specs,
            scratch_shapes=scratch,
        ),
        out_shape=out_shape,
        compiler_params=pltpu.CompilerParams(vmem_limit_bytes=VMEM_LIMIT),
        cost_estimate=pl.CostEstimate(flops=flops, bytes_accessed=10**7, transcendentals=0),
        name=name,
    )(*args)


anywhere = pl.BlockSpec(memory_space=pl.ANY)


def fetch(pieces, dest, sems):
    copies = [pltpu.make_async_copy(p, dest.at[k], sems.at[k]) for k, p in enumerate(pieces)]
    for copy in copies:
        copy.start()
    for copy in copies:
        copy.wait()


def fixed(shape):
    return pl.BlockSpec(shape, lambda *at: (0,) * len(shape))


KEEP, TAKE, PLACE, CORE = range(4)


def own_slot(flags, slot):
    return jnp.minimum(slot, flags[KEEP] - 1)


def is_live(flags, slot):
    return slot < flags[KEEP] + flags[TAKE]


def live_at(flags, slot, block, blocks):
    live = flags[KEEP] + flags[TAKE]
    return jnp.minimum(slot, live - 1), jnp.where(slot < live, block, blocks - 1)


def result_slot(flags, slot, steps):
    after = jnp.clip(slot - flags[TAKE], flags[KEEP] - 1, steps - 1)
    return jnp.where(slot < flags[KEEP], slot, after)


def kinds(flags, slot, steps):
    own = slot < flags[KEEP]
    far = (slot == flags[KEEP]) & (flags[TAKE] > 0)
    return own, far, jnp.logical_not(own | far) & (slot - flags[TAKE] < steps)


def pack_body(ada, qkv, out, up, down, bias, first, second, first_s, second_s):
    rows, width = out.shape
    me = lax.axis_index("dp").astype(jnp.int32)
    first_s[...] = jnp.zeros_like(first_s)
    second_s[...] = jnp.zeros_like(second_s)

    def put(dest, start, ref):
        for part in range(ref.shape[1] // width):
            dest[start + part * rows : start + (part + 1) * rows] = ref[
                :, part * width : (part + 1) * width
            ].astype(f32)

    put(first_s, 0, ada)
    put(first_s, 6 * rows, qkv)
    put(second_s, 0, out)
    put(second_s, rows, up)
    after = rows + up.shape[1] * rows // width
    second_s[after : after + down.shape[0]] = down[...].astype(f32)
    source = lax.broadcasted_iota(jnp.int32, (bias.shape[1], width), 0)
    lane = lax.broadcasted_iota(jnp.int32, (bias.shape[1], width), 1)
    start = 0
    for i, count in enumerate((6 * rows, rows, up.shape[1] * rows // width, rows)):
        at = lax.rem(me * count, width) + source - start
        at = jnp.where(at >= width, at - width, at)
        hit = (source >= start) & (source < start + count) & (at == lane)
        first_s[9 * rows + i : 9 * rows + i + 1] = dot(bias[...], jnp.where(hit, 1.0, 0.0).astype(bf16))
        start += count
    first[...] = first_s[...].astype(bf16)
    second[...] = second_s[...].astype(bf16)


def pack_shards(*args):
    _, _, out, up, down, _ = args
    rows, width = out.shape
    sizes = (up_to(9 * rows + 4, 16), up_to(rows + up.shape[1] * rows // width + down.shape[0] + 4, 16))
    return pl.pallas_call(
        pack_body,
        out_shape=[shape_of((n, width), bf16) for n in sizes],
        scratch_shapes=[pltpu.VMEM((n, width), f32) for n in sizes],
        name="pack_shards",
    )(*args)


def each_shard(flags, chips, blocks_of):
    first = flags[CORE] == 0
    for chip in range(chips):
        mine, other = blocks_of(jnp.bitwise_xor(flags[PLACE], chip_order(chip, chips)))
        mine, other = mine.astype(f32), other.astype(f32)
        yield 2 * chip, jnp.where(first, mine, other)
        yield 2 * chip + 1, jnp.where(first, other, mine)


def place_columns(dest, device, block, start, rows, count, width):
    for part in range(count):
        dest[device * rows : (device + 1) * rows, part * width : (part + 1) * width] = block[
            start + part * rows : start + (part + 1) * rows
        ]


def attend_pair(qkv, pair, expo, att, inv):
    length = att.shape[-2]
    row_block = 256
    keys = qkv[0, 1, pair]
    values = qkv[0, 2, pair]
    values_ones = jnp.concatenate([values, jnp.ones_like(values)], 1)
    first = lax.broadcasted_iota(jnp.int32, (row_block, PAIR), 1) < HEAD
    for i in range(length // row_block):
        r = pl.ds(i * row_block, row_block)
        query = qkv[0, 0, pair, r, :]
        outs = []
        for head in range(2):
            sel = first if head == 0 else jnp.logical_not(first)
            scores = dot(jnp.where(sel, query, jnp.zeros_like(query)), keys, 1, 1)
            top = jnp.max(scores, -1, keepdims=True)
            e = jnp.exp2((scores - top) * (0.125 * LOG2E)).astype(bf16)
            expo[0, head, r, :] = e
            outs.append(dot(e, values_ones))
        out = jnp.where(first, outs[0][:, :PAIR], outs[1][:, :PAIR])
        inverse = 1.0 / jnp.where(first, outs[0][:, PAIR:], outs[1][:, PAIR:])
        att[0, 0, r, :] = (out * inverse).astype(bf16)
        inv[0, 0, r, :] = inverse


def attend_forward_body(flags, own_x, far_x, cond, *refs):
    pieces = refs[:-11]
    qkv, expo, att, inv, mod, bias, w_qkv, w_f32, bias_f32, shards, sems = refs[-11:]
    slot = pl.program_id(0)
    pair = pl.program_id(1)
    length, width = own_x.shape[1:]
    group, others = shards.shape[1:3]
    chips = group * others
    rows = width // (2 * chips)
    pairs = width // PAIR

    def blocks_of(place):
        at = lax.div(place, others), lax.rem(place, others)
        return shards[(0, *at)], shards[(1, *at)]

    @pl.when((slot == 0) & (pair == 0))
    def _():
        fetch(pieces[:group], shards.at[0], sems.at[0])
        fetch(pieces[group:], shards.at[1], sems.at[1])
        bias_f32[...] = jnp.zeros_like(bias_f32)
        lane = lax.broadcasted_iota(jnp.int32, (1, width), 1)
        for device, block in each_shard(flags, chips, blocks_of):
            place_columns(w_f32, device, block, 0, rows, 6, width)
            start = 0
            for i, count in enumerate((6 * rows, rows, bias_f32.shape[0] * rows - 8 * rows, rows)):
                low, high = device * count, (device + 1) * count
                for part in range(low // width, (high - 1) // width + 1):
                    at = lane + part * width
                    bias_f32[start + part : start + part + 1] += jnp.where(
                        (at >= low) & (at < high), block[9 * rows + i : 9 * rows + i + 1], 0.0
                    )
                start += 2 * chips * count // width
        for part in range(6):
            cols = slice(part * width, (part + 1) * width)
            mod[:, cols] = dot(cond[...], w_f32[:, cols].astype(bf16)) + bias_f32[part : part + 1]
        for part in range(bias_f32.shape[0] - 6):
            bias[:, part * width : (part + 1) * width] = bias_f32[6 + part : 7 + part]
        for device, block in each_shard(flags, chips, blocks_of):
            place_columns(w_f32, device, block, 6 * rows, rows, 3, width)
        w_qkv[...] = w_f32[:, : 3 * width].astype(bf16)

    @pl.when((pair == 0) & is_live(flags, slot))
    def _():
        shift = mod[pl.ds(slot, 1), :width]
        scale = 1.0 + mod[pl.ds(slot, 1), width : 2 * width]
        row_block = 256

        def project(ref):
            @pl.loop(0, length // row_block)
            def _(i):
                r = pl.ds(pl.multiple_of(i * row_block, row_block), row_block)
                normed, _ = norm(ref[0, r, :].astype(f32))
                h1 = (normed * scale + shift).astype(bf16)
                result = dot(h1, w_qkv[...]).astype(bf16)
                for kind in range(3):
                    for p in range(pairs):
                        at = kind * width + p * PAIR
                        qkv[0, kind, p, r, :] = result[:, at : at + PAIR]

        @pl.when(slot < flags[KEEP])
        def _():
            project(own_x)

        @pl.when(slot >= flags[KEEP])
        def _():
            project(far_x)

    @pl.when(is_live(flags, slot))
    def _():
        attend_pair(qkv, pair, expo, att, inv)


def attend_forward(flags, own_x, far_x, cond, mine, other, bias_rows):
    steps, length, width = own_x.shape
    pairs = width // PAIR
    shards_shape = (2, len(mine)) + mine[0].shape
    args = (flags, own_x, far_x, cond, *mine, *other)

    def at(s, p, flags):
        return live_at(flags, s, p, pairs) + (0, 0)

    whole = pl.BlockSpec((1, 3, pairs, length, PAIR), lambda s, p, flags: (at(s, p, flags)[0], 0, 0, 0, 0))
    part = pl.BlockSpec((1, 1, length, PAIR), at)
    return call(
        attend_forward_body,
        (steps, pairs),
        [
            pl.BlockSpec((1, length, width), lambda s, p, flags: (own_slot(flags, s), 0, 0)),
            fixed(far_x.shape), fixed(cond.shape),
        ] + [anywhere] * (2 * len(mine)),
        [
            whole,
            pl.BlockSpec((1, 2, length, length), at),
            part, part,
            fixed((8, 6 * width)), fixed((1, (bias_rows - 6) * width)), fixed((width, 3 * width)),
        ],
        [
            shape_of((steps, 3, pairs, length, PAIR), bf16),
            shape_of((steps, 2 * pairs, length, length), bf16),
            shape_of((steps, pairs, length, PAIR), bf16),
            shape_of((steps, pairs, length, PAIR), f32),
            shape_of((8, 6 * width), f32),
            shape_of((1, (bias_rows - 6) * width), f32),
            shape_of((width, 3 * width), bf16),
        ],
        [
            pltpu.VMEM((width, 6 * width), f32),
            pltpu.VMEM((bias_rows, width), f32),
            pltpu.VMEM(shards_shape, bf16),
            pltpu.SemaphoreType.DMA((2, len(mine))),
        ],
        "attend_forward", 30 * 10**9, args,
    )


def pack_chunk(flags, device, chunk, keep, send):
    place = jnp.bitwise_xor(flags[PLACE], chip_order(device >> 1, keep.shape[0]))

    @pl.when(flags[CORE] == (device & 1))
    def _():
        keep[place] = chunk[...].astype(keep.dtype)

    @pl.when(flags[CORE] != (device & 1))
    def _():
        send[place] = chunk[...].astype(bf16)


def feed_forward_body(
    steps, flags, own_x, far_x, own_g, far_g, att, inv, mod, bias, *refs
):
    (
        own_out, far_out, grad_x1, grad_att, note, keep, send,
        x_s, g_s, w_out, w_up, w_down, sum_out, sum_up, sum_down_t, down_f32, chunk, bias_sum,
        grad_mod, note_s, shards, sems,
    ) = refs[-22:]
    pieces = refs[:-22]
    slot = pl.program_id(0)
    step = pl.program_id(1)
    own, far, dead = kinds(flags, slot, steps)
    width = x_s.shape[1]
    hidden_units = w_up.shape[1]
    ratio = hidden_units // width
    group, _, others = shards.shape[:3]
    chips = group * others
    rows = width // (2 * chips)

    def blocks_of(place):
        part, place = lax.div(place, others), lax.rem(place, others)
        return shards[part, 0, place], shards[part, 1, place]

    @pl.when((slot == 0) & (step == 0))
    def _():
        fetch(pieces, shards, sems)
        for device, block in each_shard(flags, chips, blocks_of):
            place_columns(sum_out, device, block, 0, rows, 1, width)
            place_columns(sum_up, device, block, rows, rows, ratio, width)
            place_columns(
                down_f32, device, block, (1 + ratio) * rows, ratio * rows, 1, width
            )
        w_out[...] = sum_out[...].astype(bf16)
        w_up[...] = sum_up[...].astype(bf16)
        w_down[...] = down_f32[...].astype(bf16)
        for ref in (sum_out, sum_up, sum_down_t, bias_sum, chunk, grad_mod):
            ref[...] = jnp.zeros_like(ref)

    @pl.when(dead)
    def _():
        own_out[...] = jnp.zeros_like(own_out)

    @pl.when(own)
    def _():
        x_s[...] = own_x[0].astype(f32)
        g_s[...] = own_g[0].astype(f32)

    @pl.when(far)
    def _():
        x_s[...] = far_x[0].astype(f32)
        g_s[...] = far_g[0].astype(f32)

    @pl.when(is_live(flags, slot))
    def _():
        def vector(part):
            return mod[pl.ds(slot, 1), part * width : (part + 1) * width]

        gate1, shift2, scale2, gate2 = vector(2), vector(3), 1.0 + vector(4), vector(5)
        b_out = bias[:, :width]
        b_up = bias[:, width : width + hidden_units]
        b_down = bias[:, width + hidden_units :]

        def lanes(ref):
            return jnp.concatenate([ref[0, p] for p in range(ref.shape[1])], 1)

        attended = lanes(att)
        branch1 = dot(attended, w_out[...]) + b_out
        x1 = x_s[...] + gate1 * branch1
        normed2, rstd = norm(x1)
        h2 = (normed2 * scale2 + shift2).astype(bf16)
        pre = dot(h2, w_up[...]) + b_up
        cdf = 0.5 * (1.0 + lax.erf(pre * (1 / math.sqrt(2.0))))
        hidden = (pre * cdf).astype(bf16)
        slope = cdf + pre * jnp.exp2(pre * pre * (-0.5 * LOG2E)) * (1 / math.sqrt(2 * math.pi))
        branch2 = dot(hidden, w_down[...]) + b_down
        result = (x1 + gate2 * branch2).astype(bf16)

        @pl.when(own)
        def _():
            own_out[0] = result

        @pl.when(far)
        def _():
            far_out[0] = result

        grad = g_s[...]
        grad_b2 = (gate2 * grad).astype(bf16)
        grad_pre = (dot(grad_b2, w_down[...], 1, 1) * slope).astype(bf16)
        grad_h2 = dot(grad_pre, w_up[...], 1, 1)
        grad_n = grad_h2 * scale2
        g_x1 = grad + rstd * (
            grad_n
            - jnp.mean(grad_n, -1, keepdims=True)
            - normed2 * jnp.mean(grad_n * normed2, -1, keepdims=True)
        )
        grad_b1 = (gate1 * g_x1).astype(bf16)
        grad_x1[0] = g_x1
        g_att = (dot(grad_b1, w_out[...], 1, 1) * lanes(inv)).astype(bf16)
        for p in range(width // PAIR):
            grad_att[0, p] = g_att[:, p * PAIR : (p + 1) * PAIR]

        def add_mod(part, value):
            grad_mod[pl.ds(slot, 1), part * width : (part + 1) * width] += row_sum(value)

        add_mod(0, g_x1 * branch1)
        add_mod(1, grad_h2)
        add_mod(2, grad_h2 * normed2)
        add_mod(3, grad * branch2)
        sum_out[...] += dot(attended, grad_b1, 0, 0)
        sum_up[...] += dot(h2, grad_pre, 0, 0)
        sum_down_t[...] += dot(grad_b2, hidden, 0, 0)
        bias_sum[:, :width] += row_sum(grad_b1.astype(f32))
        bias_sum[:, width : width + hidden_units] += row_sum(grad_pre.astype(f32))
        bias_sum[:, width + hidden_units :] += row_sum(grad_b2.astype(f32))

    @pl.when((slot == pl.num_programs(0) - 1) & (step == pl.num_programs(1) - 1))
    def _():
        down_f32[...] = sum_down_t[...].T
        for device in range(2 * chips):
            span = slice(device * rows, (device + 1) * rows)
            chunk[:rows] = sum_out[span]
            for part in range(ratio):
                chunk[(1 + part) * rows : (2 + part) * rows] = sum_up[
                    span, part * width : (part + 1) * width
                ]
            chunk[(1 + ratio) * rows : (1 + 2 * ratio) * rows] = down_f32[
                device * ratio * rows : (device + 1) * ratio * rows
            ]
            up_row = 1 + device * ratio * rows // width
            for i, part in enumerate((0, up_row, 1 + ratio)):
                at = (1 + 2 * ratio) * rows + i
                chunk[at : at + 1] = bias_sum[:, part * width : (part + 1) * width]
            pack_chunk(flags, device, chunk, keep, send)
        note_s[...] = jnp.zeros_like(note_s)
        for row in range(4 * steps):
            part = row % 4
            note_s[row : row + 1] = grad_mod[
                row // 4 : row // 4 + 1, part * width : (part + 1) * width
            ]
        note[...] = note_s[...].astype(bf16)


def feed_forward(
    flags, own_x, far_x, own_g, far_g, att, inv, mod, bias, shards, hidden_units
):
    steps, length, width = own_x.shape
    row_block = 1024
    blocks = length // row_block
    group, others = len(shards), shards[0].shape[1]
    rows = width // (2 * group * others)
    ratio = hidden_units // width
    packed_rows = up_to((1 + 2 * ratio) * rows + 3, 16)
    sum_shape = (group * others, packed_rows, width)
    note_shape = (up_to(4 * steps, 16), width)

    def own(s, b, flags):
        return (own_slot(flags, s), jnp.where(s < flags[KEEP], b, blocks - 1), 0)

    def far(s, b, flags):
        keep = flags[KEEP]
        return (0, jnp.where(s < keep, 0, jnp.where(s == keep, b, blocks - 1)), 0)

    def live(s, b, flags):
        return live_at(flags, s, b, blocks) + (0,)

    def live_parts(s, b, flags):
        at, part = live_at(flags, s, b, blocks)
        return (at, 0, part, 0)

    def own_result(s, b, flags):
        own, _, dead = kinds(flags, s, steps)
        return (result_slot(flags, s, steps), jnp.where(own | dead, b, blocks - 1), 0)

    def block(where):
        return pl.BlockSpec((1, row_block, width), where)

    def parts(count):
        return pl.BlockSpec((1, count, row_block, PAIR), live_parts)

    pairs = width // PAIR
    args = (flags, own_x, far_x, own_g, far_g, att, inv, mod, bias, *shards)
    return call(
        functools.partial(feed_forward_body, steps),
        (steps + 1, blocks),
        [
            block(own), block(far), block(own), block(far), parts(pairs), parts(pairs),
            fixed(mod.shape), fixed(bias.shape),
        ] + [anywhere] * group,
        [
            block(own_result), block(far), block(live), parts(pairs),
            fixed(note_shape), fixed(sum_shape), fixed(sum_shape),
        ],
        [
            shape_of((steps, length, width), bf16),
            shape_of((1, length, width), bf16),
            shape_of((steps, length, width), f32),
            shape_of((steps, pairs, length, PAIR), bf16),
            shape_of(note_shape, bf16),
            shape_of(sum_shape, bf16),
            shape_of(sum_shape, bf16),
        ],
        [
            pltpu.VMEM((row_block, width), f32),
            pltpu.VMEM((row_block, width), f32),
            pltpu.VMEM((width, width), bf16),
            pltpu.VMEM((width, hidden_units), bf16),
            pltpu.VMEM((hidden_units, width), bf16),
            pltpu.VMEM((width, width), f32),
            pltpu.VMEM((width, hidden_units), f32),
            pltpu.VMEM((width, hidden_units), f32),
            pltpu.VMEM((hidden_units, width), f32),
            pltpu.VMEM((packed_rows, width), f32),
            pltpu.VMEM(bias.shape, f32),
            pltpu.VMEM((8, 4 * width), f32),
            pltpu.VMEM(note_shape, f32),
            pltpu.VMEM((group,) + shards[0].shape, bf16),
            pltpu.SemaphoreType.DMA((group,)),
        ],
        "feed_forward", 60 * 10**9, args,
    )


def attend_backward_pair(qkv, expo, att, grad_att, g_qkv, keys_t, values_t):
    length = att.shape[2]
    row_block = 512
    keys = qkv[0, 1, 0]
    values = qkv[0, 2, 0]
    values_ones = jnp.concatenate([values, jnp.ones_like(values)], 1)
    lane = lax.broadcasted_iota(jnp.int32, (row_block, PAIR), 1)
    first = lane < HEAD
    for i in range(length // row_block):
        r = pl.ds(i * row_block, row_block)
        query = qkv[0, 0, 0, r, :]
        g_att = grad_att[0, 0, r, :]
        product = g_att.astype(f32) * att[0, 0, r, :].astype(f32)
        query_t = query.T
        g_att_t = g_att.T
        grads_q = []
        for head in range(2):
            sel = first if head == 0 else jnp.logical_not(first)
            delta = jnp.sum(jnp.where(sel, product, 0.0), -1, keepdims=True)
            high = delta.astype(bf16).astype(f32)
            extra = jnp.where(
                lane == 0, -high, jnp.where(lane == 1, high - delta, 0.0)
            ).astype(bf16)
            left = jnp.concatenate([jnp.where(sel, g_att, jnp.zeros_like(g_att)), extra], 1)
            e = expo[0, head, r, :]
            grad_s = e * dot(left, values_ones, 1, 1).astype(bf16)
            grads_q.append(dot(grad_s, keys))
            span = slice(head * HEAD, (head + 1) * HEAD)
            add_k = dot(query_t[span], grad_s)
            add_v = dot(g_att_t[span], e)
            if i == 0:
                keys_t[span] = add_k
                values_t[span] = add_v
            else:
                keys_t[span] += add_k
                values_t[span] += add_v
        g_qkv[0, r, :] = (jnp.where(first, grads_q[0], grads_q[1]) * 0.125).astype(bf16)
    g_qkv[1] = (keys_t[...] * 0.125).astype(bf16).T
    g_qkv[2] = values_t[...].astype(bf16).T


def first_pairs_body(flags, qkv, expo, att, grad_att, g_qkv, keys_t, values_t):
    @pl.when(is_live(flags, pl.program_id(0)))
    def _():
        attend_backward_pair(qkv, expo, att, grad_att, g_qkv.at[0, 0], keys_t, values_t)


def first_pairs(flags, qkv, expo, att, grad_att):
    steps, _, pairs, length, _ = qkv.shape
    pairs -= 1

    def part(s, p, flags):
        return live_at(flags, s, p, pairs) + (0, 0)

    def qkv_at(s, p, flags):
        at, pair = live_at(flags, s, p, pairs)
        return (at, 0, pair, 0, 0)

    heads = pl.BlockSpec((1, 1, length, PAIR), part)
    return call(
        first_pairs_body,
        (steps, pairs),
        [
            pl.BlockSpec((1, 3, 1, length, PAIR), qkv_at),
            pl.BlockSpec((1, 2, length, length), part),
            heads, heads,
        ],
        pl.BlockSpec((1, 1, 3, length, PAIR), lambda s, p, flags: part(s, p, flags) + (0,)),
        shape_of((steps, pairs, 3, length, PAIR), bf16),
        [pltpu.VMEM((PAIR, length), f32), pltpu.VMEM((PAIR, length), f32)],
        "first_pairs", 40 * 10**9, (flags, qkv, expo, att, grad_att),
    )


def finish_body(
    steps, flags, own_x, far_x, qkv, expo, att, grad_att, grad_x1, mod, w_qkv, g_first,
    own_grad, far_grad, note, keep, send, g_last, keys_t, values_t, sum_qkv, chunk, grad_mod, note_s,
):
    slot = pl.program_id(0)
    own, far, dead = kinds(flags, slot, steps)
    length, width = own_x.shape[1:]
    chips = keep.shape[0]
    rows = width // (2 * chips)

    @pl.when(slot == 0)
    def _():
        for ref in (sum_qkv, chunk, grad_mod):
            ref[...] = jnp.zeros_like(ref)

    @pl.when(dead)
    def _():
        own_grad[...] = jnp.zeros_like(own_grad)

    @pl.when(is_live(flags, slot))
    def _():
        attend_backward_pair(qkv, expo, att, grad_att, g_last, keys_t, values_t)

    def finish(x_ref, out_ref):
        shift = mod[pl.ds(slot, 1), :width]
        scale = 1.0 + mod[pl.ds(slot, 1), width : 2 * width]
        row_block = 512
        for i in range(length // row_block):
            r = pl.ds(i * row_block, row_block)
            normed, rstd = norm(x_ref[0, r, :].astype(f32))
            h1 = (normed * scale + shift).astype(bf16)
            grad = []
            for kind in range(3):
                grad += [g_first[0, p, kind, r, :] for p in range(g_first.shape[1])]
                grad.append(g_last[kind, r, :])
            grad = jnp.concatenate(grad, 1)
            grad_h1 = dot(grad, w_qkv[...], 1, 1)
            sum_qkv[...] += dot(h1, grad, 0, 0)
            grad_mod[pl.ds(slot, 1), :width] += row_sum(grad_h1)
            grad_mod[pl.ds(slot, 1), width:] += row_sum(grad_h1 * normed)
            grad_n = grad_h1 * scale
            out_ref[0, r, :] = (
                grad_x1[0, r, :]
                + rstd
                * (
                    grad_n
                    - jnp.mean(grad_n, -1, keepdims=True)
                    - normed * jnp.mean(grad_n * normed, -1, keepdims=True)
                )
            ).astype(out_ref.dtype)

    @pl.when(own)
    def _():
        finish(own_x, own_grad)

    @pl.when(far)
    def _():
        finish(far_x, far_grad)

    @pl.when(slot == steps)
    def _():
        for device in range(2 * chips):
            for part in range(3):
                chunk[part * rows : (part + 1) * rows] = sum_qkv[
                    device * rows : (device + 1) * rows, part * width : (part + 1) * width
                ]
            pack_chunk(flags, device, chunk, keep, send)
        note_s[...] = jnp.zeros_like(note_s)
        for row in range(2 * steps):
            part = row % 2
            note_s[row : row + 1] = grad_mod[
                row // 2 : row // 2 + 1, part * width : (part + 1) * width
            ]
        note[...] = note_s[...].astype(bf16)


def finish(
    flags, own_x, far_x, qkv, expo, att, grad_att, grad_x1, mod, w_qkv, g_first, chips
):
    steps, length, width = own_x.shape
    last = width // PAIR - 1
    sum_shape = (chips, up_to(3 * width // (2 * chips), 8), width)
    note_shape = (up_to(2 * steps, 8), width)

    def at(*part):
        return lambda s, flags: (live_at(flags, s, 0, 1)[0],) + part

    def block(where):
        return pl.BlockSpec((1, length, width), where)

    heads = pl.BlockSpec((1, 1, length, PAIR), at(last, 0, 0))
    return call(
        functools.partial(finish_body, steps),
        (steps + 1,),
        [
            block(lambda s, flags: (own_slot(flags, s), 0, 0)),
            block(lambda s, flags: (0, 0, 0)),
            pl.BlockSpec((1, 3, 1, length, PAIR), at(0, last, 0, 0)),
            pl.BlockSpec((1, 2, length, length), at(last, 0, 0)),
            heads, heads, block(at(0, 0)), fixed(mod.shape), fixed(w_qkv.shape),
            pl.BlockSpec((1, last, 3, length, PAIR), at(0, 0, 0, 0)),
        ],
        [
            block(lambda s, flags: (result_slot(flags, s, steps), 0, 0)),
            block(lambda s, flags: (0, 0, 0)),
            fixed(note_shape), fixed(sum_shape), fixed(sum_shape),
        ],
        [
            shape_of((steps, length, width), f32),
            shape_of((1, length, width), bf16),
            shape_of(note_shape, bf16),
            shape_of(sum_shape, f32),
            shape_of(sum_shape, bf16),
        ],
        [
            pltpu.VMEM((3, length, PAIR), bf16),
            pltpu.VMEM((PAIR, length), f32),
            pltpu.VMEM((PAIR, length), f32),
            pltpu.VMEM((width, 3 * width), f32),
            pltpu.VMEM(sum_shape[1:], f32),
            pltpu.VMEM((8, 2 * width), f32),
            pltpu.VMEM(note_shape, f32),
        ],
        "finish", 40 * 10**9,
        (flags, own_x, far_x, qkv, expo, att, grad_att, grad_x1, mod, w_qkv, g_first),
    )


def swap(array, mask):
    count = lax.axis_size("dp")
    return lax.ppermute(array, "dp", [(i, i ^ mask) for i in range(count)])


def tie(value, *others):
    return lax.optimization_barrier((value,) + others)[0]


def chip_groups(chips):
    bits = chips.bit_length() - 1
    return tuple(tuple(range(max(top - 2, 0), top)) for top in range(bits, 0, -2))


def chip_order(chip, chips):
    place, low = 0, 0
    for group in chip_groups(chips):
        place = place | ((chip >> group[0]) & ((1 << len(group)) - 1)) << low
        low += len(group)
    return place


def group_masks(group):
    return [sum(((k >> i) & 1) << b for i, b in enumerate(group)) for k in range(1, 1 << len(group))]


def gather_group(held, group):
    return [held] + [swap(held, mask << 1) for mask in group_masks(group)]


def stage_body(adds, sends, with_notes, held, notes, *refs):
    adds, outs = refs[:adds], refs[adds:]
    parts, rows, _ = held.shape
    size = parts * rows
    keep, joined, outs = outs[0], outs[1], outs[2:]
    own = notes.shape[0]
    joined[:own] = notes[...]
    if adds[0].shape[0] > size:
        for k, add in enumerate(adds):
            joined[(k + 1) * own : (k + 2) * own] = add[size:]
    count = parts // (sends + 1)
    for part in range(parts):
        total = held[part].astype(f32)
        for add in adds:
            total = total + add[part * rows : (part + 1) * rows].astype(f32)
        if part < count:
            keep[part] = total
        else:
            at = part % count * rows
            outs[part // count - 1][at : at + rows] = total.astype(bf16)
    if with_notes:
        for out in outs:
            out[count * rows :] = joined[...]


def stage(held, notes, adds, sends=0, with_notes=True):
    parts, rows, width = held.shape
    extra = adds[0].shape[0] - parts * rows
    count = parts // (sends + 1)
    joined = notes.shape[0] + len(adds) * extra
    size = count * rows + (joined if with_notes else 0)
    keep, joined, *outs = pl.pallas_call(
        functools.partial(stage_body, len(adds), sends, with_notes),
        out_shape=[shape_of((count, rows, width), f32), shape_of((joined, width), bf16)]
        + [shape_of((size, width), bf16)] * sends,
        name="stage",
    )(held, notes, *adds)
    return keep, joined, outs


def reduce_start(group, sums, notes):
    masks = group_masks(group)
    parts = [held.shape[0] // (len(masks) + 1) for held in sums]
    got = []
    for k, mask in enumerate(masks):
        pieces = [held[(k + 1) * n : (k + 2) * n].astype(bf16) for held, n in zip(sums, parts)]
        pieces += notes
        width = pieces[0].shape[-1]
        got.append(swap(jnp.concatenate([p.reshape(-1, width) for p in pieces], 0), mask << 1))
    return [held[:part] for held, part in zip(sums, parts)], notes, got


def reduce_done(totals, notes, got, *after):
    got = lax.optimization_barrier(tuple(got) + after)[: len(got)]
    joined = [[note] for note in notes]
    for block in got:
        start = 0
        for i, piece in enumerate(totals + notes):
            size = math.prod(piece.shape[:-1])
            part = block[start : start + size].reshape(piece.shape)
            start += size
            if i < len(totals):
                totals = totals[:i] + [totals[i] + part.astype(f32)] + totals[i + 1 :]
            else:
                joined[i - len(totals)].append(part)
    return totals, [jnp.concatenate(blocks, 0) for blocks in joined]


def hand_back_body(at, back_out, back_grad, _out, _grad, _after, out, grad, done, low, high, sems):
    done[...] = jnp.zeros_like(done)

    @pl.when(at[0] > 0)
    def _():
        loads = [
            pltpu.make_async_copy(back_grad.at[0], low.at[0], sems.at[0]),
            pltpu.make_async_copy(back_out.at[0], low.at[1], sems.at[1]),
        ]
        for load in loads:
            load.start()
        loads[0].wait()
        high[...] = low[0].astype(f32)
        loads[1].wait()
        stores = [
            pltpu.make_async_copy(high, grad.at[at[1]], sems.at[2]),
            pltpu.make_async_copy(low.at[1], out.at[at[1]], sems.at[3]),
        ]
        for store in stores:
            store.start()
        for store in stores:
            store.wait()


def hand_back(at, back_out, back_grad, own_out, own_grad, after):
    return pl.pallas_call(
        hand_back_body,
        grid_spec=pltpu.PrefetchScalarGridSpec(
            num_scalar_prefetch=1,
            grid=(1,),
            in_specs=[anywhere] * 5,
            out_specs=[anywhere] * 2 + [fixed((8, 128))],
            scratch_shapes=[
                pltpu.VMEM((2,) + own_grad.shape[1:], bf16),
                pltpu.VMEM(own_grad.shape[1:], f32),
                pltpu.SemaphoreType.DMA((4,)),
            ],
        ),
        out_shape=[
            shape_of(own_out.shape, bf16), shape_of(own_grad.shape, f32), shape_of((8, 128), f32),
        ],
        input_output_aliases={3: 0, 4: 1},
        name="hand_back",
    )(at, back_out, back_grad, own_out, own_grad, after)


def condition_body(at, steps, order, *refs):
    pieces, (left, blocks, cond, sems) = refs[:-4], refs[-4:]
    width = cond.shape[1]
    rows = width * steps // cond.shape[0]
    me = lax.axis_index("dp").astype(jnp.int32)
    base = at // 16 * 16
    fetch([piece.at[:, :, pl.ds(base, 16), :] for piece in pieces], blocks, sems)
    at -= base
    for core in range(2):
        for place, (part, other) in enumerate(order):
            start = (core * len(order) + place) * steps
            cond[start : start + steps] = blocks[part, core, other, at : at + steps].astype(f32)
    turned = pltpu.roll(cond[...], lax.rem(width - me * rows, width), 1)[:, :PAIR]
    lane = lax.broadcasted_iota(jnp.int32, turned.shape, 1)
    left[...] = jnp.where(lane < rows, turned, jnp.where(lane == rows, 1.0, 0.0)).astype(bf16)


def condition_columns(pieces, sizes, cond_row, steps):
    _, others, _, width = pieces[0].shape
    chips = len(pieces) * others
    order = []
    for place in range(chips):
        digits, rest = [], place
        for size in sizes:
            digits.append(rest % size)
            rest //= size
        other, low = 0, 1
        for digit, size in zip(reversed(digits[1:]), reversed(sizes[1:])):
            other += digit * low
            low *= size
        order.append((digits[0], other))
    return pl.pallas_call(
        functools.partial(condition_body, cond_row, steps, order),
        in_specs=[anywhere] * len(pieces),
        out_shape=shape_of((2 * chips * steps, PAIR), bf16),
        scratch_shapes=[
            pltpu.VMEM((len(pieces), 2, others, 16, width), bf16),
            pltpu.VMEM((2 * chips * steps, width), f32),
            pltpu.SemaphoreType.DMA((len(pieces),)),
        ],
        name="condition_columns",
    )(*pieces)


def result_body(
    sums1, sums2, left, mine1, other1, mine2, other2, _done,
    ada, b_ada, qkv, out, b_out, up, b_up, down, b_down, ada_sum,
):
    rows, width = out.shape
    ratio = up.shape[1] // width
    me = lax.axis_index("dp").astype(jnp.int32)
    for part in range(3):
        qkv[:, part * width : (part + 1) * width] = sums1[0, part * rows : (part + 1) * rows]
    out[...] = sums2[0, :rows]
    for part in range(ratio):
        up[:, part * width : (part + 1) * width] = sums2[
            0, (1 + part) * rows : (2 + part) * rows
        ]
    after = (1 + 2 * ratio) * rows
    down[...] = sums2[0, after - ratio * rows : after]
    for i, ref in enumerate((b_out, b_up, b_down)):
        size = ref.shape[1]
        line = sums2[0, after + i : after + i + 1]
        shift = lax.rem(width - lax.rem(me * size, width), width)
        ref[...] = pltpu.roll(line, shift, 1)[:, :size]
    half = left.shape[0] // 2
    start = 0
    for count, refs in ((2, (mine1, other1)), (4, (mine2, other2))):
        source = lax.broadcasted_iota(jnp.int32, (half, count * half), 1)
        target = lax.broadcasted_iota(jnp.int32, (half, count * half), 0)
        for part in range(count):
            pick = jnp.where(source == target * count + part, 1.0, 0.0).astype(bf16)
            total = 0.0
            for i, ref in enumerate(refs):
                picked = dot(pick, ref[...]).astype(bf16)
                total = total + dot(left[i * half : (i + 1) * half], picked, 0, 0)
            cols = slice((start + part) * width, (start + part + 1) * width)
            ada[:, cols] = total[:rows]
            ada_sum[:, cols] = total[rows : rows + 1]
        start += count
    b_ada[...] = pltpu.roll(ada_sum[...], lax.rem(6 * width - me * 6 * rows, 6 * width), 1)[
        :, : 6 * rows
    ]


def results(sums1, sums2, left, mine1, other1, mine2, other2, done, rows, ratio):
    width = sums1.shape[2]
    shapes = [
        (rows, 6 * width), (1, 6 * rows), (rows, 3 * width), (rows, width), (1, rows),
        (rows, ratio * width), (1, ratio * rows), (ratio * rows, width), (1, rows),
    ]
    return pl.pallas_call(
        result_body,
        out_shape=[shape_of(s, f32) for s in shapes],
        scratch_shapes=[pltpu.VMEM((1, 6 * width), f32)],
        name="results",
    )(sums1, sums2, left, mine1, other1, mine2, other2, done)


def body(
    fields, conditions, step_counts, cotangent,
    w_ada, b_ada, w_qkv, w_out, b_out, w_up, b_up, w_down, b_down,
):
    devices = lax.axis_size("dp")
    chips = devices // 2
    me = lax.axis_index("dp").astype(jnp.int32)
    chip, core = me >> 1, me & 1
    steps, length, width = fields.shape[1:]
    hidden_units = w_up.shape[1]
    ratio = hidden_units // width
    rows = width // devices
    fields, conditions, cotangent = fields[0], conditions[0], cotangent[0]
    groups = chip_groups(chips)

    count = step_counts[0]
    biases = jnp.concatenate([b_ada, b_out, b_up, b_down])[None]
    first, second = pack_shards(w_ada, w_qkv, w_out, w_up, w_down, biases)
    head = jnp.concatenate([conditions, jnp.full((4, width), count, bf16)], 0)
    other_head = swap(tie(head, first), 1)
    other_count = other_head[steps, 0].astype(jnp.int32)
    give = count - other_count >= 2
    take = (other_count - count >= 2).astype(jnp.int32)
    keep = count - give.astype(jnp.int32)
    flags = jnp.stack([keep, take, chip_order(chip, chips), core])
    far_cond = lax.dynamic_index_in_dim(other_head, other_count - 1, 0)
    cond = jnp.concatenate([conditions, jnp.zeros((8 - steps, width), bf16)], 0)
    cond = jnp.where((jnp.arange(8) == keep)[:, None] & (take > 0), far_cond, cond)
    cond_act = jax.nn.silu(cond.astype(f32)).astype(bf16)

    cond_row = (1 + 2 * ratio) * rows
    mine_a = first[None]
    mine_b = lax.dynamic_update_slice_in_dim(second, cond_act[:steps], cond_row, 0)[None]
    for group in groups[:-1]:
        pieces = lax.optimization_barrier((*gather_group(mine_a, group), cond_act, flags))[:-2]
        mine_a = jnp.concatenate(pieces, 0)
    far_x = swap(tie(lax.dynamic_index_in_dim(fields, count - 1, 0), mine_a), 1)
    far_g = swap(tie(lax.dynamic_index_in_dim(cotangent, count - 1, 0), mine_a), 1)
    for group in groups[:-1]:
        mine_b = jnp.concatenate(gather_group(tie(mine_b, far_x, far_g), group), 0)
    both_b = jnp.stack([mine_b, swap(tie(mine_b, mine_a), 1)])
    mine_a = gather_group(mine_a, groups[-1])
    other_a = [swap(piece, 1) for piece in mine_a]
    back_at = jnp.stack([give.astype(jnp.int32), count - 1])
    first_kernel = lax.optimization_barrier(
        (flags, both_b, far_x, far_g, cond_act, back_at)
    )
    back_at = first_kernel[5]
    qkv, expo, att, inv, mod, bias, full_qkv = attend_forward(
        first_kernel[0], fields, far_x, cond_act, mine_a, other_a, 8 + ratio
    )
    all_b = gather_group(first_kernel[1], groups[-1])
    all_b = lax.optimization_barrier((*all_b, mod))[:-1]
    own_out, far_out, grad_x1, grad_att, note2, keep2, send2 = feed_forward(
        flags, fields, far_x, cotangent, far_g, att, inv, mod, bias, all_b, hidden_units
    )

    up_groups = tuple(reversed(groups))
    late = up_groups[2:]
    masks = [[mask << 1 for mask in group_masks(group)] for group in up_groups]
    left = condition_columns(all_b, [len(m) + 1 for m in masks], cond_row, steps)
    got2 = tie(swap(send2.reshape(-1, width), 1), left)
    held2, note2, sends = stage(keep2, note2, [got2], len(masks[0]))
    gots = [swap(send, mask) for send, mask in zip(sends, masks[0])]
    back_out = swap(far_out, 1)
    g_first = first_pairs(tie(flags, held2), qkv, expo, att, grad_att)
    gots = lax.optimization_barrier((*gots, g_first))[:-1]
    held2, note2, sends = stage(held2, note2, gots, len(masks[1]))
    gots = [swap(send, mask) for send, mask in zip(sends, masks[1])]
    own_grad, far_grad, note1, keep1, send1 = finish(
        tie(flags, held2, back_out), fields, far_x, qkv, expo, att, grad_att, grad_x1, mod, full_qkv, g_first,
        chips,
    )
    got1 = swap(send1, 1)
    gots = lax.optimization_barrier((*gots, keep1))[:-1]
    held2, note2, sends = stage(held2, note2, gots, len(masks[2]) if late else 0)
    held1 = keep1 + got1.astype(f32)
    back_grad = swap(far_grad, 1)
    note1 = note1[None]

    going = reduce_start(up_groups[0], [held1], [note1])
    (held1,), (note1,) = reduce_done(*going, back_grad)
    own_out, own_grad, done = hand_back(
        back_at, back_out, back_grad, own_out, own_grad, held1
    )
    for i, group in enumerate(up_groups[1:]):
        if i > 0:
            gots = [swap(send, mask) for send, mask in zip(sends, masks[i + 1])]
            held2, note2, sends = stage(
                held2, note2, gots, len(masks[i + 2]) if i + 2 < len(masks) else 0
            )
        (held1,), (note1,) = reduce_done(*reduce_start(group, [held1], [note1]))
    note1 = note1.reshape(-1, width)
    other1, other2 = swap(note1, 1), swap(note2, 1)
    grads = results(held1, held2, left, note1, other1, note2, other2, done, rows, ratio)
    grads = [g[0] if i in (1, 4, 6, 8) else g for i, g in enumerate(grads)]

    return (own_out[None], own_grad[None], *grads)


def solution(mesh):
    item, matrix, vector = P("dp", None, None, None), P("dp", None), P("dp")
    return jax.shard_map(
        body,
        mesh=mesh,
        in_specs=(
            item, P("dp", None, None), vector, item,
            matrix, vector, matrix, matrix, vector, matrix, vector, matrix, vector,
        ),
        out_specs=(
            item, item, matrix, vector, matrix, matrix, vector, matrix, vector, matrix, vector,
        ),
        check_vma=False,
    )
```

profile of v0, /device:TPU:0, one launch (start us, length us, event | category | flops | bytes accessed | tf_op | source)
XLA Modules:
  0.0 293.0 jit_solution(11718642025828866995)
XLA Ops:
  2.0 1.8 pack_shards.1
  3.8 5.1 %collective-permute-start.3 = (bf16[1,112,384]{2,1,0:T(8,128)(2,1)}, bf16[1,112,384]{2,1,0:T(8,128)(2,1)S(1)}, u32[]{:S(2)}, u32[]{:S(2)}) collective-permute-start(bf16[1,112,384]{2,1,0:T(8,128)(2,1)} %bitcast.101), channel_id=1, source_target_pairs={{0,24},{1,25},{2,26},{3,27},{4,28},{5,29},{6,30},{7,31},{8,16},{9,... | collective-permute-start | bytes 258056 | tf_op jit(solution)/shard_map/ppermute | solution.py:738
  10.9 1.5 dynamic-slice_bitcast_fusion
  14.5 1.9 collective-permute-done.2
  17.0 2.5 collective-permute-start.12
  20.6 2.7 collective-permute-start.8
  23.3 5.0 %collective-permute-done.6 = bf16[1,112,384]{2,1,0:T(8,128)(2,1)S(1)} collective-permute-done((bf16[1,112,384]{2,1,0:T(8,128)(2,1)S(1)}, bf16[1,112,384]{2,1,0:T(8,128)(2,1)S(1)}, u32[]{:S(2)}, u32[]{:S(2)}) %collective-permute-start.6) | collective-permute-done | bytes 86048 | tf_op jit(solution)/shard_map/ppermute | solution.py:738
  28.8 5.8 %collective-permute-done.7 = bf16[1,112,384]{2,1,0:T(8,128)(2,1)S(1)} collective-permute-done((bf16[1,112,384]{2,1,0:T(8,128)(2,1)S(1)}, bf16[1,112,384]{2,1,0:T(8,128)(2,1)S(1)}, u32[]{:S(2)}, u32[]{:S(2)}) %collective-permute-start.7) | collective-permute-done | bytes 86048 | tf_op jit(solution)/shard_map/ppermute | solution.py:738
  36.6 2.5 collective-permute-start.19
  41.7 35.0 %attend_forward.1 = (bf16[4,3,3,1024,128]{4,3,2,1,0:T(8,128)(2,1)}, bf16[4,6,1024,1024]{3,2,1,0:T(8,128)(2,1)}, bf16[4,3,1024,128]{3,2,1,0:T(8,128)(2,1)}, f32[4...) custom-call(s32[4]{0:T(128)} %pad_add_fusion.flags, ...), custom_call_target="tpu_custom_call" | custom-call | flops 30000001024 | bytes 10000000 | tf_op jit(solution)/shard_map/attend_forward/pallas_call | solution.py:44
  78.1 49.8 %feed_forward.1 = (bf16[4,1024,384]{2,1,0:T(8,128)(2,1)}, bf16[1,1024,384]{2,1,0:T(8,128)(2,1)}, f32[4,1024,384]{2,1,0:T(8,128)}, bf16[4,3,1024,128]{3,2,1,0:T(8...) custom-call(s32[4]{0:T(128)} %pad_add_fusion.flags, ...), custom_call_target="tpu_custom_call" | custom-call | flops 60000002048 | bytes 10000000 | tf_op jit(solution)/shard_map/feed_forward/pallas_call | solution.py:44
  128.0 24.4 %collective-permute-start.21 = (bf16[1792,384]{1,0:T(8,128)(2,1)}, bf16[1792,384]{1,0:T(8,128)(2,1)S(1)}, u32[]{:S(2)}, u32[]{:S(2)}) collective-permute-start(bf16[1792,384]{1,0:T(8,128)(2,1)} %bitcast.108), channel_id=1, source_target_pairs={{0,1},{1,0},{2,3},{3,2},{4,5},{5,4},{6,7},{7,6},{8,9},{9,8},{10,11... | collective-permute-start | bytes 4128776 | tf_op jit(solution)/shard_map/ppermute | solution.py:738
  152.4 1.8 condition_columns.1.left
  156.4 3.1 %stage.3 = (f32[4,112,384]{2,1,0:T(8,128)}, bf16[16,384]{1,0:T(8,128)(2,1)}, bf16[464,384]{1,0:T(8,128)(2,1)}, bf16[464,384]{1,0:T(8,128)(2,1)}, bf16[464,384]{1,0:T(8,128)(2,1)}) custom-call(bf16[16,112,384]{2,1,0:T(8,128)(2,1)} %get-tuple-element.110.held, bf16[16,384]{1,0:T(8,128)(2,1)} %get-tuple-element.111.notes, bf16[1792,384]{1,0:T(8,128)(2,1)} %copy-done.1), custom_call_target="tpu_custom_call" | custom-call | tf_op jit(solution)/shard_map/stage/pallas_call | solution.py:797
  159.5 2.3 collective-permute-start.22
  161.8 1.5 collective-permute-start.23
  163.3 20.7 %first_pairs.1.g_first = bf16[4,2,3,1024,128]{4,3,2,1,0:T(8,128)(2,1)} custom-call(s32[4]{0:T(128)} %pad_add_fusion.flags, bf16[4,3,3,1024,128]{4,3,2,1,0:T(8,128)(2,1)} %get-tuple-element.120.qkv, bf16[4,6,1024,1024]{3,2,1,0:T(8,128)(2,1)} %get-tuple-element.121.expo, bf16[4,3,1024,128]{3,2,1,0:T(8,128)(2,1)} %get-tuple-element.100.att, ...), custom_call_target="tpu_custom_call" | custom-call | flops 40000000000 | bytes 10000000 | tf_op jit(solution)/shard_map/first_pairs/pallas_call | solution.py:44
  184.9 2.3 stage.4
  187.2 23.2 %finish.1 = (f32[4,1024,384]{2,1,0:T(8,128)}, bf16[1,1024,384]{2,1,0:T(8,128)(2,1)}, bf16[8,384]{1,0:T(8,128)(2,1)}, f32[16,40,384]{2,1,0:T(8,128)}, bf16[16,40,384]{2,1,0:T(8,128)(2,1)}) custom-call(s32[4]{0:T(128)} %pad_add_fusion.flags, bf16[4,1024,384]{2,1,0:T(8,128)(2,1)} %bitcast.97, bf16[1,1024,384]{2,1,0:T(8,128)(2,1)} %copy-done.22, ...), custom_call_target="tpu_custom_call" | custom-call | flops 40000000000 | bytes 10000000 | tf_op jit(solution)/shard_map/finish/pallas_call | solution.py:44
  210.4 13.8 %collective-permute-start.26 = (bf16[16,40,384]{2,1,0:T(8,128)(2,1)}, bf16[16,40,384]{2,1,0:T(8,128)(2,1)S(1)}, u32[]{:S(2)}, u32[]{:S(2)}) collective-permute-start(bf16[16,40,384]{2,1,0:T(8,128)(2,1)} %get-tuple-element.134), channel_id=1, source_target_pairs={{0,1},{1,0},{2,3},{3,2},{4,5},{5,4},{6,7},{7,6},{8,9},{9,8},{10,11... | collective-permute-start | bytes 1474568 | tf_op jit(solution)/shard_map/ppermute | solution.py:738
  224.3 11.2 %collective-permute-start.33 = (bf16[176,384]{1,0:T(8,128)(2,1)S(1)}, bf16[176,384]{1,0:T(8,128)(2,1)S(1)}, u32[]{:S(2)}, u32[]{:S(2)}) collective-permute-start(bf16[176,384]{1,0:T(8,128)(2,1)S(1)} %copy-done.30), channel_id=1, source_target_pairs={{0,8},{1,9},{2,10},{3,11},{4,12},{5,13},{6,14},{7,15},{8,0},{9,1},... | collective-permute-start | bytes 405512 | tf_op jit(solution)/shard_map/ppermute | solution.py:738
  235.4 2.4 collective-permute-start.35
  239.3 1.5 collective-permute-start.29
  240.8 29.0 %collective-permute-start.28 = (bf16[168,384]{1,0:T(8,128)(2,1)S(1)}, bf16[168,384]{1,0:T(8,128)(2,1)S(1)}, u32[]{:S(2)}, u32[]{:S(2)}) collective-permute-start(bf16[168,384]{1,0:T(8,128)(2,1)S(1)} %get-tuple-element.177), channel_id=1, source_target_pairs={{0,4},{1,5},{2,6},{3,7},{4,0},{5,1},{6,2},{7,3},{8,12},{9,13},{10,... | collective-permute-start | bytes 387080 | tf_op jit(solution)/shard_map/ppermute | solution.py:738
  271.8 1.9 stage.5
  273.7 2.1 collective-permute-done.28
  275.8 1.9 collective-permute-done.27
  278.7 1.5 collective-permute-start.32
  281.3 1.9 collective-permute-start.30
  285.2 1.8 collective-permute-done.31
  287.1 1.5 fusion.3.sums1
  289.3 3.5 %results.1 = (f32[12,2304]{1,0:T(8,128)}, f32[1,72]{1,0:T(1,128)}, f32[12,1152]{1,0:T(8,128)}, f32[12,384]{1,0:T(8,128)}, f32[1,12]{1,0:T(1,128)}, /*index=5*/f3...) custom-call(f32[1,40,384]{2,1,0:T(8,128)} %fusion.3.sums1, ...), custom_call_target="tpu_custom_call" | custom-call | tf_op jit(solution)/shard_map/results/pallas_call | solution.py:971
  (158 shorter events, 23.5 us)
Async XLA Ops:
  3.8 10.7 %collective-permute-start.3 = (bf16[1,112,384]{2,1,0:T(8,128)(2,1)}, bf16[1,112,384]{2,1,0:T(8,128)(2,1)S(1)}, u32[]{:S(2)}, u32[]{:S(2)}) collective-permute-start(bf16[1,112,384]{2,1,0:T(8,128)(2,1)} %bitcast.101), channel_id=1, source_target_pairs={{0,24},{1,25},{2,26},{3,27},{4,28},{5,29},{6,30},{7,31},{8,16},{9,... | collective-permute-start | bytes 258056 | tf_op jit(solution)/shard_map/ppermute | solution.py:738
  8.9 7.4 %collective-permute-start.2 = (bf16[1,112,384]{2,1,0:T(8,128)(2,1)}, bf16[1,112,384]{2,1,0:T(8,128)(2,1)S(1)}, u32[]{:S(2)}, u32[]{:S(2)}) collective-permute-start(bf16[1,112,384]{2,1,0:T(8,128)(2,1)} %bitcast.102), channel_id=1, source_target_pairs={{0,16},{1,17},{2,18},{3,19},{4,20},{5,21},{6,22},{7,23},{8,24},{9,... | collective-permute-start | bytes 258056 | tf_op jit(solution)/shard_map/ppermute | solution.py:738
  8.9 7.4 %collective-permute-start.1 = (bf16[1,112,384]{2,1,0:T(8,128)(2,1)}, bf16[1,112,384]{2,1,0:T(8,128)(2,1)S(1)}, u32[]{:S(2)}, u32[]{:S(2)}) collective-permute-start(bf16[1,112,384]{2,1,0:T(8,128)(2,1)} %bitcast.103), channel_id=1, source_target_pairs={{0,8},{1,9},{2,10},{3,11},{4,12},{5,13},{6,14},{7,15},{8,0},{9,1},... | collective-permute-start | bytes 258056 | tf_op jit(solution)/shard_map/ppermute | solution.py:738
  17.0 18.3 %collective-permute-start.12 = (bf16[4,112,384]{2,1,0:T(8,128)(2,1)S(1)}, bf16[4,112,384]{2,1,0:T(8,128)(2,1)S(1)}, u32[]{:S(2)}, u32[]{:S(2)}) collective-permute-start(bf16[4,112,384]{2,1,0:T(8,128)(2,1)S(1)} %constant_dynamic-update-slice_fusion.refs_0_), channel_id=1, source_target_pairs={{0,6},{1,7},{2,4},{3,5},{4,2},{5,3},{6,0},{7,1},{8,14},{9,15},{10,... | collective-permute-start | bytes 1032200 | tf_op jit(solution)/shard_map/ppermute | solution.py:738
  19.5 15.9 %collective-permute-start.11 = (bf16[4,112,384]{2,1,0:T(8,128)(2,1)S(1)}, bf16[4,112,384]{2,1,0:T(8,128)(2,1)S(1)}, u32[]{:S(2)}, u32[]{:S(2)}) collective-permute-start(bf16[4,112,384]{2,1,0:T(8,128)(2,1)S(1)} %constant_dynamic-update-slice_fusion.refs_0_), channel_id=1, source_target_pairs={{0,4},{1,5},{2,6},{3,7},{4,0},{5,1},{6,2},{7,3},{8,12},{9,13},{10,... | collective-permute-start | bytes 1032200 | tf_op jit(solution)/shard_map/ppermute | solution.py:738
  20.0 15.8 %collective-permute-start.10 = (bf16[4,112,384]{2,1,0:T(8,128)(2,1)S(1)}, bf16[4,112,384]{2,1,0:T(8,128)(2,1)S(1)}, u32[]{:S(2)}, u32[]{:S(2)}) collective-permute-start(bf16[4,112,384]{2,1,0:T(8,128)(2,1)S(1)} %constant_dynamic-update-slice_fusion.refs_0_), channel_id=1, source_target_pairs={{0,2},{1,3},{2,0},{3,1},{4,6},{5,7},{6,4},{7,5},{8,10},{9,11},{10,... | collective-permute-start | bytes 1032200 | tf_op jit(solution)/shard_map/ppermute | solution.py:738
  20.6 14.1 %collective-permute-start.8 = (bf16[1,112,384]{2,1,0:T(8,128)(2,1)S(1)}, bf16[1,112,384]{2,1,0:T(8,128)(2,1)S(1)}, u32[]{:S(2)}, u32[]{:S(2)}) collective-permute-start(bf16[1,112,384]{2,1,0:T(8,128)(2,1)S(1)} %fusion.8), channel_id=1, source_target_pairs={{0,24},{1,25},{2,26},{3,27},{4,28},{5,29},{6,30},{7,31},{8,16},{9,... | collective-permute-start | bytes 258056 | tf_op jit(solution)/shard_map/ppermute | solution.py:738
  23.3 5.1 %collective-permute-start.6 = (bf16[1,112,384]{2,1,0:T(8,128)(2,1)S(1)}, bf16[1,112,384]{2,1,0:T(8,128)(2,1)S(1)}, u32[]{:S(2)}, u32[]{:S(2)}) collective-permute-start(bf16[1,112,384]{2,1,0:T(8,128)(2,1)S(1)} %fusion.8), channel_id=1, source_target_pairs={{0,8},{1,9},{2,10},{3,11},{4,12},{5,13},{6,14},{7,15},{8,0},{9,1},... | collective-permute-start | bytes 258056 | tf_op jit(solution)/shard_map/ppermute | solution.py:738
  28.4 6.3 %collective-permute-start.7 = (bf16[1,112,384]{2,1,0:T(8,128)(2,1)S(1)}, bf16[1,112,384]{2,1,0:T(8,128)(2,1)S(1)}, u32[]{:S(2)}, u32[]{:S(2)}) collective-permute-start(bf16[1,112,384]{2,1,0:T(8,128)(2,1)S(1)} %fusion.8), channel_id=1, source_target_pairs={{0,16},{1,17},{2,18},{3,19},{4,20},{5,21},{6,22},{7,23},{8,24},{9,... | collective-permute-start | bytes 258056 | tf_op jit(solution)/shard_map/ppermute | solution.py:738
  35.3 4.3 %collective-permute-start.16 = (bf16[4,112,384]{2,1,0:T(8,128)(2,1)S(1)}, bf16[4,112,384]{2,1,0:T(8,128)(2,1)}, u32[]{:S(2)}, u32[]{:S(2)}) collective-permute-start(bf16[4,112,384]{2,1,0:T(8,128)(2,1)S(1)} %collective-permute-done.12.refs_3_), channel_id=1, source_target_pairs={{0,1},{1,0},{2,3},{3,2},{4,5},{5,4},{6,7},{7,6},{8,9},{9,8},{10,11... | collective-permute-start | bytes 1032200 | tf_op jit(solution)/shard_map/ppermute | solution.py:738
  35.4 4.8 %collective-permute-start.15 = (bf16[4,112,384]{2,1,0:T(8,128)(2,1)S(1)}, bf16[4,112,384]{2,1,0:T(8,128)(2,1)S(1)}, u32[]{:S(2)}, u32[]{:S(2)}) collective-permute-start(bf16[4,112,384]{2,1,0:T(8,128)(2,1)S(1)} %collective-permute-done.11.refs_2_), channel_id=1, source_target_pairs={{0,1},{1,0},{2,3},{3,2},{4,5},{5,4},{6,7},{7,6},{8,9},{9,8},{10,11... | collective-permute-start | bytes 1032200 | tf_op jit(solution)/shard_map/ppermute | solution.py:738
  35.8 4.4 %collective-permute-start.14 = (bf16[4,112,384]{2,1,0:T(8,128)(2,1)S(1)}, bf16[4,112,384]{2,1,0:T(8,128)(2,1)S(1)}, u32[]{:S(2)}, u32[]{:S(2)}) collective-permute-start(bf16[4,112,384]{2,1,0:T(8,128)(2,1)S(1)} %collective-permute-done.10.refs_1_), channel_id=1, source_target_pairs={{0,1},{1,0},{2,3},{3,2},{4,5},{5,4},{6,7},{7,6},{8,9},{9,8},{10,11... | collective-permute-start | bytes 1032200 | tf_op jit(solution)/shard_map/ppermute | solution.py:738
  36.6 40.1 %collective-permute-start.19 = (bf16[2,4,112,384]{3,2,1,0:T(8,128)(2,1)S(1)}, bf16[2,4,112,384]{3,2,1,0:T(8,128)(2,1)S(1)}, u32[]{:S(2)}, u32[]{:S(2)}) collective-permute-start(bf16[2,4,112,384]{3,2,1,0:T(8,128)(2,1)S(1)} %pad_maximum_fusion.refs_0_), channel_id=1, source_target_pairs={{0,6},{1,7},{2,4},{3,5},{4,2},{5,3},{6,0},{7,1},{8,14},{9,15},{10,... | collective-permute-start | bytes 2064392 | tf_op jit(solution)/shard_map/ppermute | solution.py:738
  39.1 37.7 %collective-permute-start.18 = (bf16[2,4,112,384]{3,2,1,0:T(8,128)(2,1)S(1)}, bf16[2,4,112,384]{3,2,1,0:T(8,128)(2,1)S(1)}, u32[]{:S(2)}, u32[]{:S(2)}) collective-permute-start(bf16[2,4,112,384]{3,2,1,0:T(8,128)(2,1)S(1)} %pad_maximum_fusion.refs_0_), channel_id=1, source_target_pairs={{0,4},{1,5},{2,6},{3,7},{4,0},{5,1},{6,2},{7,3},{8,12},{9,13},{10,... | collective-permute-start | bytes 2064392 | tf_op jit(solution)/shard_map/ppermute | solution.py:738
  39.6 37.1 %collective-permute-start.17 = (bf16[2,4,112,384]{3,2,1,0:T(8,128)(2,1)S(1)}, bf16[2,4,112,384]{3,2,1,0:T(8,128)(2,1)S(1)}, u32[]{:S(2)}, u32[]{:S(2)}) collective-permute-start(bf16[2,4,112,384]{3,2,1,0:T(8,128)(2,1)S(1)} %pad_maximum_fusion.refs_0_), channel_id=1, source_target_pairs={{0,2},{1,3},{2,0},{3,1},{4,6},{5,7},{6,4},{7,5},{8,10},{9,11},{10,... | collective-permute-start | bytes 2064392 | tf_op jit(solution)/shard_map/ppermute | solution.py:738
  128.0 27.4 %collective-permute-start.21 = (bf16[1792,384]{1,0:T(8,128)(2,1)}, bf16[1792,384]{1,0:T(8,128)(2,1)S(1)}, u32[]{:S(2)}, u32[]{:S(2)}) collective-permute-start(bf16[1792,384]{1,0:T(8,128)(2,1)} %bitcast.108), channel_id=1, source_target_pairs={{0,1},{1,0},{2,3},{3,2},{4,5},{5,4},{6,7},{7,6},{8,9},{9,8},{10,11... | collective-permute-start | bytes 4128776 | tf_op jit(solution)/shard_map/ppermute | solution.py:738
  154.2 33.0 %collective-permute-start.20 = (bf16[1,1024,384]{2,1,0:T(8,128)(2,1)}, bf16[1,1024,384]{2,1,0:T(8,128)(2,1)S(1)}, u32[]{:S(2)}, u32[]{:S(2)}) collective-permute-start(bf16[1,1024,384]{2,1,0:T(8,128)(2,1)} %get-tuple-element.109), channel_id=1, source_target_pairs={{0,1},{1,0},{2,3},{3,2},{4,5},{5,4},{6,7},{7,6},{8,9},{9,8},{10,11... | collective-permute-start | bytes 2359304 | tf_op jit(solution)/shard_map/ppermute | solution.py:738
  159.5 24.4 %collective-permute-start.22 = (bf16[464,384]{1,0:T(8,128)(2,1)}, bf16[464,384]{1,0:T(8,128)(2,1)S(1)}, u32[]{:S(2)}, u32[]{:S(2)}) collective-permute-start(bf16[464,384]{1,0:T(8,128)(2,1)} %get-tuple-element.116), channel_id=1, source_target_pairs={{0,2},{1,3},{2,0},{3,1},{4,6},{5,7},{6,4},{7,5},{8,10},{9,11},{10,... | collective-permute-start | bytes 1069064 | tf_op jit(solution)/shard_map/ppermute | solution.py:738
  161.8 22.2 %collective-permute-start.23 = (bf16[464,384]{1,0:T(8,128)(2,1)}, bf16[464,384]{1,0:T(8,128)(2,1)S(1)}, u32[]{:S(2)}, u32[]{:S(2)}) collective-permute-start(bf16[464,384]{1,0:T(8,128)(2,1)} %get-tuple-element.117), channel_id=1, source_target_pairs={{0,4},{1,5},{2,6},{3,7},{4,0},{5,1},{6,2},{7,3},{8,12},{9,13},{10,... | collective-permute-start | bytes 1069064 | tf_op jit(solution)/shard_map/ppermute | solution.py:738
  163.3 20.7 %collective-permute-start.24 = (bf16[464,384]{1,0:T(8,128)(2,1)}, bf16[464,384]{1,0:T(8,128)(2,1)S(1)}, u32[]{:S(2)}, u32[]{:S(2)}) collective-permute-start(bf16[464,384]{1,0:T(8,128)(2,1)} %get-tuple-element.118), channel_id=1, source_target_pairs={{0,6},{1,7},{2,4},{3,5},{4,2},{5,3},{6,0},{7,1},{8,14},{9,15},{10,... | collective-permute-start | bytes 1069064 | tf_op jit(solution)/shard_map/ppermute | solution.py:738
  210.4 27.4 %collective-permute-start.26 = (bf16[16,40,384]{2,1,0:T(8,128)(2,1)}, bf16[16,40,384]{2,1,0:T(8,128)(2,1)S(1)}, u32[]{:S(2)}, u32[]{:S(2)}) collective-permute-start(bf16[16,40,384]{2,1,0:T(8,128)(2,1)} %get-tuple-element.134), channel_id=1, source_target_pairs={{0,1},{1,0},{2,3},{3,2},{4,5},{5,4},{6,7},{7,6},{8,9},{9,8},{10,11... | collective-permute-start | bytes 1474568 | tf_op jit(solution)/shard_map/ppermute | solution.py:738
  224.3 16.6 %collective-permute-start.33 = (bf16[176,384]{1,0:T(8,128)(2,1)S(1)}, bf16[176,384]{1,0:T(8,128)(2,1)S(1)}, u32[]{:S(2)}, u32[]{:S(2)}) collective-permute-start(bf16[176,384]{1,0:T(8,128)(2,1)S(1)} %copy-done.30), channel_id=1, source_target_pairs={{0,8},{1,9},{2,10},{3,11},{4,12},{5,13},{6,14},{7,15},{8,0},{9,1},... | collective-permute-start | bytes 405512 | tf_op jit(solution)/shard_map/ppermute | solution.py:738
  235.4 34.4 %collective-permute-start.34 = (bf16[176,384]{1,0:T(8,128)(2,1)S(1)}, bf16[176,384]{1,0:T(8,128)(2,1)S(1)}, u32[]{:S(2)}, u32[]{:S(2)}) collective-permute-start(bf16[176,384]{1,0:T(8,128)(2,1)S(1)} %copy-done.29), channel_id=1, source_target_pairs={{0,16},{1,17},{2,18},{3,19},{4,20},{5,21},{6,22},{7,23},{8,24},{9,... | collective-permute-start | bytes 405512 | tf_op jit(solution)/shard_map/ppermute | solution.py:738
  235.4 35.7 %collective-permute-start.35 = (bf16[176,384]{1,0:T(8,128)(2,1)S(1)}, bf16[176,384]{1,0:T(8,128)(2,1)S(1)}, u32[]{:S(2)}, u32[]{:S(2)}) collective-permute-start(bf16[176,384]{1,0:T(8,128)(2,1)S(1)} %copy-done.28), channel_id=1, source_target_pairs={{0,24},{1,25},{2,26},{3,27},{4,28},{5,29},{6,30},{7,31},{8,16},{9,... | collective-permute-start | bytes 405512 | tf_op jit(solution)/shard_map/ppermute | solution.py:738
  237.9 39.8 %collective-permute-start.25 = (bf16[1,1024,384]{2,1,0:T(8,128)(2,1)}, bf16[1,1024,384]{2,1,0:T(8,128)(2,1)S(1)}, u32[]{:S(2)}, u32[]{:S(2)}) collective-permute-start(bf16[1,1024,384]{2,1,0:T(8,128)(2,1)} %get-tuple-element.130), channel_id=1, source_target_pairs={{0,1},{1,0},{2,3},{3,2},{4,5},{5,4},{6,7},{7,6},{8,9},{9,8},{10,11... | collective-permute-start | bytes 2359304 | tf_op jit(solution)/shard_map/ppermute | solution.py:738
  239.3 34.4 %collective-permute-start.29 = (bf16[168,384]{1,0:T(8,128)(2,1)S(1)}, bf16[168,384]{1,0:T(8,128)(2,1)S(1)}, u32[]{:S(2)}, u32[]{:S(2)}) collective-permute-start(bf16[168,384]{1,0:T(8,128)(2,1)S(1)} %get-tuple-element.176), channel_id=1, source_target_pairs={{0,6},{1,7},{2,4},{3,5},{4,2},{5,3},{6,0},{7,1},{8,14},{9,15},{10,... | collective-permute-start | bytes 387080 | tf_op jit(solution)/shard_map/ppermute | solution.py:738
  240.8 35.0 %collective-permute-start.28 = (bf16[168,384]{1,0:T(8,128)(2,1)S(1)}, bf16[168,384]{1,0:T(8,128)(2,1)S(1)}, u32[]{:S(2)}, u32[]{:S(2)}) collective-permute-start(bf16[168,384]{1,0:T(8,128)(2,1)S(1)} %get-tuple-element.177), channel_id=1, source_target_pairs={{0,4},{1,5},{2,6},{3,7},{4,0},{5,1},{6,2},{7,3},{8,12},{9,13},{10,... | collective-permute-start | bytes 387080 | tf_op jit(solution)/shard_map/ppermute | solution.py:738
  269.8 7.8 %collective-permute-start.27 = (bf16[168,384]{1,0:T(8,128)(2,1)S(1)}, bf16[168,384]{1,0:T(8,128)(2,1)S(1)}, u32[]{:S(2)}, u32[]{:S(2)}) collective-permute-start(bf16[168,384]{1,0:T(8,128)(2,1)S(1)} %get-tuple-element.178), channel_id=1, source_target_pairs={{0,2},{1,3},{2,0},{3,1},{4,6},{5,7},{6,4},{7,5},{8,10},{9,11},{10,... | collective-permute-start | bytes 387080 | tf_op jit(solution)/shard_map/ppermute | solution.py:738
  273.7 14.9 %collective-permute-start.37 = (bf16[256,384]{1,0:T(8,128)(2,1)}, bf16[256,384]{1,0:T(8,128)(2,1)S(1)}, u32[]{:S(2)}, u32[]{:S(2)}) collective-permute-start(bf16[256,384]{1,0:T(8,128)(2,1)} %get-tuple-element.152.mine2), channel_id=1, source_target_pairs={{0,1},{1,0},{2,3},{3,2},{4,5},{5,4},{6,7},{7,6},{8,9},{9,8},{10,11... | collective-permute-start | bytes 589832 | tf_op jit(solution)/shard_map/ppermute | solution.py:738
  278.7 6.5 %collective-permute-start.32 = (bf16[72,384]{1,0:T(8,128)(2,1)S(1)}, bf16[72,384]{1,0:T(8,128)(2,1)S(1)}, u32[]{:S(2)}, u32[]{:S(2)}) collective-permute-start(bf16[72,384]{1,0:T(8,128)(2,1)S(1)} %get-tuple-element.173), channel_id=1, source_target_pairs={{0,24},{1,25},{2,26},{3,27},{4,28},{5,29},{6,30},{7,31},{8,16},{9,... | collective-permute-start | bytes 165896 | tf_op jit(solution)/shard_map/ppermute | solution.py:738
  280.2 6.7 %collective-permute-start.31 = (bf16[72,384]{1,0:T(8,128)(2,1)S(1)}, bf16[72,384]{1,0:T(8,128)(2,1)S(1)}, u32[]{:S(2)}, u32[]{:S(2)}) collective-permute-start(bf16[72,384]{1,0:T(8,128)(2,1)S(1)} %get-tuple-element.174), channel_id=1, source_target_pairs={{0,16},{1,17},{2,18},{3,19},{4,20},{5,21},{6,22},{7,23},{8,24},{9,... | collective-permute-start | bytes 165896 | tf_op jit(solution)/shard_map/ppermute | solution.py:738
  281.3 5.7 %collective-permute-start.30 = (bf16[72,384]{1,0:T(8,128)(2,1)S(1)}, bf16[72,384]{1,0:T(8,128)(2,1)S(1)}, u32[]{:S(2)}, u32[]{:S(2)}) collective-permute-start(bf16[72,384]{1,0:T(8,128)(2,1)S(1)} %get-tuple-element.175), channel_id=1, source_target_pairs={{0,8},{1,9},{2,10},{3,11},{4,12},{5,13},{6,14},{7,15},{8,0},{9,1},... | collective-permute-start | bytes 165896 | tf_op jit(solution)/shard_map/ppermute | solution.py:738
  (37 other events, 418.4 us)
where the time goes:
time: 297 us; the launch traced here: 293 us
  Pallas kernels  144 us (48%)
  starting transfers between devices  110 us (37%)
  waiting for transfers between devices  20.4 us (7%)
  local copies, waits for them, and re-layouts  9.83 us (3%)
  other arithmetic  5.97 us (2%)
    pallas_call x4, Pallas kernels, call(): pl.pallas_call(body, grid_spec=pltpu.PrefetchScalarGridSpec(num_scalar_pr...  129 us
    ppermute x38, starting transfers between devices, swap(): return lax.ppermute(array, 'dp', [(i, i ^ mask) for i in range(count)])  110 us
    ppermute x38, waiting for transfers between devices, swap(): return lax.ppermute(array, 'dp', [(i, i ^ mask) for i in range(count)])  20.4 us
    pallas_call x3, Pallas kernels, stage(): pl.pallas_call(functools.partial(stage_body, len(adds), sends, with_notes...  7.23 us
    unnamed x74, local copies, waits for them, and re-layouts  6.34 us
  transfers between devices with their start and end apart: 38, of which 8 were waited for; matrix products, arithmetic and copies ran while one was open for 3% of the time, Pallas kernels for 23%

commit v1 on v0

--- a/solution.py
+++ b/solution.py
@@ -12,7 +12,7 @@
 PAIR = 2 * HEAD
 EPS = 1e-6
 LOG2E = 1.4426950408889634
-VMEM_LIMIT = 60 * 2**20
+VMEM_LIMIT = 63 * 2**20
 bf16 = jnp.bfloat16
 f32 = jnp.float32
 shape_of = jax.ShapeDtypeStruct
@@ -99,7 +99,7 @@
     return own, far, jnp.logical_not(own | far) & (slot - flags[TAKE] < steps)
 
 
-def pack_body(ada, qkv, out, up, down, bias, first, second, first_s, second_s):
+def pack_body(ada, qkv, out, up, down, b_ada, b_out, b_up, b_down, first, second, first_s, second_s):
     rows, width = out.shape
     me = lax.axis_index("dp").astype(jnp.int32)
     first_s[...] = jnp.zeros_like(first_s)
@@ -117,21 +117,20 @@
     put(second_s, rows, up)
     after = rows + up.shape[1] * rows // width
     second_s[after : after + down.shape[0]] = down[...].astype(f32)
-    source = lax.broadcasted_iota(jnp.int32, (bias.shape[1], width), 0)
-    lane = lax.broadcasted_iota(jnp.int32, (bias.shape[1], width), 1)
-    start = 0
-    for i, count in enumerate((6 * rows, rows, up.shape[1] * rows // width, rows)):
-        at = lax.rem(me * count, width) + source - start
-        at = jnp.where(at >= width, at - width, at)
-        hit = (source >= start) & (source < start + count) & (at == lane)
-        first_s[9 * rows + i : 9 * rows + i + 1] = dot(bias[...], jnp.where(hit, 1.0, 0.0).astype(bf16))
-        start += count
+    for i, bias in enumerate((b_ada, b_out, b_up, b_down)):
+        count = bias.shape[0]
+        source = lax.broadcasted_iota(jnp.int32, (count, width), 0)
+        lane = lax.broadcasted_iota(jnp.int32, (count, width), 1)
+        at = lax.rem(me * count, width) + source
+        hit = jnp.where(at >= width, at - width, at) == lane
+        line = jnp.broadcast_to(bias[...].astype(f32)[None], (8, count)).astype(bf16)
+        first_s[9 * rows + i : 9 * rows + i + 1] = dot(line, jnp.where(hit, 1.0, 0.0).astype(bf16))[:1]
     first[...] = first_s[...].astype(bf16)
     second[...] = second_s[...].astype(bf16)
 
 
 def pack_shards(*args):
-    _, _, out, up, down, _ = args
+    _, _, out, up, down = args[:5]
     rows, width = out.shape
     sizes = (up_to(9 * rows + 4, 16), up_to(rows + up.shape[1] * rows // width + down.shape[0] + 4, 16))
     return pl.pallas_call(
@@ -160,7 +159,7 @@
 
 def attend_pair(qkv, pair, expo, att, inv):
     length = att.shape[-2]
-    row_block = 256
+    row_block = 128
     keys = qkv[0, 1, pair]
     values = qkv[0, 2, pair]
     values_ones = jnp.concatenate([values, jnp.ones_like(values)], 1)
@@ -992,8 +991,9 @@
     groups = chip_groups(chips)
 
     count = step_counts[0]
-    biases = jnp.concatenate([b_ada, b_out, b_up, b_down])[None]
-    first, second = pack_shards(w_ada, w_qkv, w_out, w_up, w_down, biases)
+    first, second = pack_shards(
+        w_ada, w_qkv, w_out, w_up, w_down, b_ada, b_out, b_up, b_down
+    )
     head = jnp.concatenate([conditions, jnp.full((4, width), count, bf16)], 0)
     other_head = swap(tie(head, first), 1)
     other_count = other_head[steps, 0].astype(jnp.int32)

time: 297 us -> 291 us (0.980)
    unnamed x74 -> x64, local copies, waits for them, and re-layouts: 6.34 us -> 4.07 us
  transfers between devices with their start and end apart: 38 -> 38, of which waited for: 8 -> 10; matrix products, arithmetic and copies ran while one was open for 3% -> 3% of each run, Pallas kernels for 23% -> 23%
where the time goes in v1:
time: 291 us; the launch traced here: 288 us
  Pallas kernels  144 us (49%)
  starting transfers between devices  110 us (38%)
  waiting for transfers between devices  19.7 us (7%)
  local copies, waits for them, and re-layouts  6.99 us (2%)
  other arithmetic  5.12 us (2%)
    pallas_call x4, Pallas kernels, call(): pl.pallas_call(body, grid_spec=pltpu.PrefetchScalarGridSpec(num_scalar_pr...  128 us
    ppermute x38, starting transfers between devices, swap(): return lax.ppermute(array, 'dp', [(i, i ^ mask) for i in range(count)])  110 us
    ppermute x38, waiting for transfers between devices, swap(): return lax.ppermute(array, 'dp', [(i, i ^ mask) for i in range(count)])  19.7 us
    pallas_call x3, Pallas kernels, stage(): pl.pallas_call(functools.partial(stage_body, len(adds), sends, with_notes...  7.23 us
  transfers between devices with their start and end apart: 38, of which 10 were waited for; matrix products, arithmetic and copies ran while one was open for 3% of the time, Pallas kernels for 23%

profile of v1, /device:TPU:0, one launch (start us, length us, event | category | flops | bytes accessed | tf_op | source)
XLA Modules:
  0.0 288.2 jit_solution(17885675895693458783)
XLA Ops:
  0.7 1.8 pack_shards.1
  2.5 5.1 %collective-permute-start.3 = (bf16[1,112,384]{2,1,0:T(8,128)(2,1)}, bf16[1,112,384]{2,1,0:T(8,128)(2,1)S(1)}, u32[]{:S(2)}, u32[]{:S(2)}) collective-permute-start(bf16[1,112,384]{2,1,0:T(8,128)(2,1)} %bitcast.101), channel_id=1, source_target_pairs={{0,24},{1,25},{2,26},{3,27},{4,28},{5,29},{6,30},{7,31},{8,16},{9,... | collective-permute-start | bytes 258056 | tf_op jit(solution)/shard_map/ppermute | solution.py:737
  9.6 1.5 dynamic-slice_bitcast_fusion
  13.1 1.9 collective-permute-done.2
  15.7 2.5 collective-permute-start.12
  19.3 2.7 collective-permute-start.8
  22.0 4.9 %collective-permute-done.6 = bf16[1,112,384]{2,1,0:T(8,128)(2,1)S(1)} collective-permute-done((bf16[1,112,384]{2,1,0:T(8,128)(2,1)S(1)}, bf16[1,112,384]{2,1,0:T(8,128)(2,1)S(1)}, u32[]{:S(2)}, u32[]{:S(2)}) %collective-permute-start.6) | collective-permute-done | bytes 86048 | tf_op jit(solution)/shard_map/ppermute | solution.py:737
  27.4 5.8 %collective-permute-done.7 = bf16[1,112,384]{2,1,0:T(8,128)(2,1)S(1)} collective-permute-done((bf16[1,112,384]{2,1,0:T(8,128)(2,1)S(1)}, bf16[1,112,384]{2,1,0:T(8,128)(2,1)S(1)}, u32[]{:S(2)}, u32[]{:S(2)}) %collective-permute-start.7) | collective-permute-done | bytes 86048 | tf_op jit(solution)/shard_map/ppermute | solution.py:737
  35.3 2.3 collective-permute-start.19
  40.4 34.5 %attend_forward.1 = (bf16[4,3,3,1024,128]{4,3,2,1,0:T(8,128)(2,1)}, bf16[4,6,1024,1024]{3,2,1,0:T(8,128)(2,1)}, bf16[4,3,1024,128]{3,2,1,0:T(8,128)(2,1)}, f32[4...) custom-call(s32[4]{0:T(128)} %pad_add_fusion.flags, ...), custom_call_target="tpu_custom_call" | custom-call | flops 30000001024 | bytes 10000000 | tf_op jit(solution)/shard_map/attend_forward/pallas_call | solution.py:44
  75.0 50.0 %feed_forward.1 = (bf16[4,1024,384]{2,1,0:T(8,128)(2,1)}, bf16[1,1024,384]{2,1,0:T(8,128)(2,1)}, f32[4,1024,384]{2,1,0:T(8,128)}, bf16[4,3,1024,128]{3,2,1,0:T(8...) custom-call(s32[4]{0:T(128)} %pad_add_fusion.flags, ...), custom_call_target="tpu_custom_call" | custom-call | flops 60000002048 | bytes 10000000 | tf_op jit(solution)/shard_map/feed_forward/pallas_call | solution.py:44
  125.0 1.8 condition_columns.1.left
  127.4 1.0 collective-permute-done.21.refs_0_
  128.4 1.1 copy-done.1
  129.4 3.1 %stage.3 = (f32[4,112,384]{2,1,0:T(8,128)}, bf16[16,384]{1,0:T(8,128)(2,1)}, bf16[464,384]{1,0:T(8,128)(2,1)}, bf16[464,384]{1,0:T(8,128)(2,1)}, bf16[464,384]{1,0:T(8,128)(2,1)}) custom-call(bf16[16,112,384]{2,1,0:T(8,128)(2,1)} %get-tuple-element.110.held, bf16[16,384]{1,0:T(8,128)(2,1)} %get-tuple-element.111.notes, bf16[1792,384]{1,0:T(8,128)(2,1)} %copy-done.1), custom_call_target="tpu_custom_call" | custom-call | tf_op jit(solution)/shard_map/stage/pallas_call | solution.py:796
  132.5 25.8 %collective-permute-start.22 = (bf16[464,384]{1,0:T(8,128)(2,1)}, bf16[464,384]{1,0:T(8,128)(2,1)}, u32[]{:S(2)}, u32[]{:S(2)}) collective-permute-start(bf16[464,384]{1,0:T(8,128)(2,1)} %get-tuple-element.116), channel_id=1, source_target_pairs={{0,2},{1,3},{2,0},{3,1},{4,6},{5,7},{6,4},{7,5},{8,10},{9,11},{10,... | collective-permute-start | bytes 1069064 | tf_op jit(solution)/shard_map/ppermute | solution.py:737
  158.3 23.9 %collective-permute-start.23 = (bf16[464,384]{1,0:T(8,128)(2,1)}, bf16[464,384]{1,0:T(8,128)(2,1)}, u32[]{:S(2)}, u32[]{:S(2)}) collective-permute-start(bf16[464,384]{1,0:T(8,128)(2,1)} %get-tuple-element.117), channel_id=1, source_target_pairs={{0,4},{1,5},{2,6},{3,7},{4,0},{5,1},{6,2},{7,3},{8,12},{9,13},{10,... | collective-permute-start | bytes 1069064 | tf_op jit(solution)/shard_map/ppermute | solution.py:737
  182.2 1.5 collective-permute-start.24
  183.7 20.7 %first_pairs.1.g_first = bf16[4,2,3,1024,128]{4,3,2,1,0:T(8,128)(2,1)} custom-call(s32[4]{0:T(128)} %pad_add_fusion.flags, bf16[4,3,3,1024,128]{4,3,2,1,0:T(8,128)(2,1)} %get-tuple-element.120.qkv, bf16[4,6,1024,1024]{3,2,1,0:T(8,128)(2,1)} %get-tuple-element.121.expo, bf16[4,3,1024,128]{3,2,1,0:T(8,128)(2,1)} %get-tuple-element.100.att, ...), custom_call_target="tpu_custom_call" | custom-call | flops 40000000000 | bytes 10000000 | tf_op jit(solution)/shard_map/first_pairs/pallas_call | solution.py:44
  204.3 2.3 stage.4
  206.6 23.1 %finish.1 = (f32[4,1024,384]{2,1,0:T(8,128)}, bf16[1,1024,384]{2,1,0:T(8,128)(2,1)}, bf16[8,384]{1,0:T(8,128)(2,1)}, f32[16,40,384]{2,1,0:T(8,128)}, bf16[16,40,384]{2,1,0:T(8,128)(2,1)}) custom-call(s32[4]{0:T(128)} %pad_add_fusion.flags, bf16[4,1024,384]{2,1,0:T(8,128)(2,1)} %bitcast.97, bf16[1,1024,384]{2,1,0:T(8,128)(2,1)} %copy-done.16, ...), custom_call_target="tpu_custom_call" | custom-call | flops 40000000000 | bytes 10000000 | tf_op jit(solution)/shard_map/finish/pallas_call | solution.py:44
  229.9 4.3 %collective-permute-start.35 = (bf16[176,384]{1,0:T(8,128)(2,1)S(1)}, bf16[176,384]{1,0:T(8,128)(2,1)S(1)}, u32[]{:S(2)}, u32[]{:S(2)}) collective-permute-start(bf16[176,384]{1,0:T(8,128)(2,1)S(1)} %copy-done.25), channel_id=1, source_target_pairs={{0,24},{1,25},{2,26},{3,27},{4,28},{5,29},{6,30},{7,31},{8,16},{9,... | collective-permute-start | bytes 405512 | tf_op jit(solution)/shard_map/ppermute | solution.py:737
  234.2 1.3 fusion.11
  235.7 1.0 collective-permute-start.29
  237.2 30.1 %collective-permute-start.28 = (bf16[168,384]{1,0:T(8,128)(2,1)S(1)}, bf16[168,384]{1,0:T(8,128)(2,1)S(1)}, u32[]{:S(2)}, u32[]{:S(2)}) collective-permute-start(bf16[168,384]{1,0:T(8,128)(2,1)S(1)} %get-tuple-element.177), channel_id=1, source_target_pairs={{0,4},{1,5},{2,6},{3,7},{4,0},{5,1},{6,2},{7,3},{8,12},{9,13},{10,... | collective-permute-start | bytes 387080 | tf_op jit(solution)/shard_map/ppermute | solution.py:737
  268.1 1.9 stage.5
  270.0 2.7 collective-permute-done.28
  272.7 1.3 collective-permute-done.27
  275.8 3.7 %collective-permute-start.30 = (bf16[72,384]{1,0:T(8,128)(2,1)S(1)}, bf16[72,384]{1,0:T(8,128)(2,1)S(1)}, u32[]{:S(2)}, u32[]{:S(2)}) collective-permute-start(bf16[72,384]{1,0:T(8,128)(2,1)S(1)} %get-tuple-element.175), channel_id=1, source_target_pairs={{0,8},{1,9},{2,10},{3,11},{4,12},{5,13},{6,14},{7,15},{8,0},{9,1},... | collective-permute-start | bytes 165896 | tf_op jit(solution)/shard_map/ppermute | solution.py:737
  279.5 1.3 hand_back.1
  282.3 1.5 fusion.3.sums1
  284.5 3.5 %results.1 = (f32[12,2304]{1,0:T(8,128)}, f32[1,72]{1,0:T(1,128)}, f32[12,1152]{1,0:T(8,128)}, f32[12,384]{1,0:T(8,128)}, f32[1,12]{1,0:T(1,128)}, /*index=5*/f3...) custom-call(f32[1,40,384]{2,1,0:T(8,128)} %fusion.3.sums1, ...), custom_call_target="tpu_custom_call" | custom-call | tf_op jit(solution)/shard_map/results/pallas_call | solution.py:970
  (146 shorter events, 15.8 us)
Async XLA Ops:
  2.5 10.6 %collective-permute-start.3 = (bf16[1,112,384]{2,1,0:T(8,128)(2,1)}, bf16[1,112,384]{2,1,0:T(8,128)(2,1)S(1)}, u32[]{:S(2)}, u32[]{:S(2)}) collective-permute-start(bf16[1,112,384]{2,1,0:T(8,128)(2,1)} %bitcast.101), channel_id=1, source_target_pairs={{0,24},{1,25},{2,26},{3,27},{4,28},{5,29},{6,30},{7,31},{8,16},{9,... | collective-permute-start | bytes 258056 | tf_op jit(solution)/shard_map/ppermute | solution.py:737
  7.6 7.4 %collective-permute-start.2 = (bf16[1,112,384]{2,1,0:T(8,128)(2,1)}, bf16[1,112,384]{2,1,0:T(8,128)(2,1)S(1)}, u32[]{:S(2)}, u32[]{:S(2)}) collective-permute-start(bf16[1,112,384]{2,1,0:T(8,128)(2,1)} %bitcast.102), channel_id=1, source_target_pairs={{0,16},{1,17},{2,18},{3,19},{4,20},{5,21},{6,22},{7,23},{8,24},{9,... | collective-permute-start | bytes 258056 | tf_op jit(solution)/shard_map/ppermute | solution.py:737
  7.6 7.4 %collective-permute-start.1 = (bf16[1,112,384]{2,1,0:T(8,128)(2,1)}, bf16[1,112,384]{2,1,0:T(8,128)(2,1)S(1)}, u32[]{:S(2)}, u32[]{:S(2)}) collective-permute-start(bf16[1,112,384]{2,1,0:T(8,128)(2,1)} %bitcast.103), channel_id=1, source_target_pairs={{0,8},{1,9},{2,10},{3,11},{4,12},{5,13},{6,14},{7,15},{8,0},{9,1},... | collective-permute-start | bytes 258056 | tf_op jit(solution)/shard_map/ppermute | solution.py:737
  15.7 18.1 %collective-permute-start.12 = (bf16[4,112,384]{2,1,0:T(8,128)(2,1)S(1)}, bf16[4,112,384]{2,1,0:T(8,128)(2,1)S(1)}, u32[]{:S(2)}, u32[]{:S(2)}) collective-permute-start(bf16[4,112,384]{2,1,0:T(8,128)(2,1)S(1)} %constant_dynamic-update-slice_fusion.refs_0_), channel_id=1, source_target_pairs={{0,6},{1,7},{2,4},{3,5},{4,2},{5,3},{6,0},{7,1},{8,14},{9,15},{10,... | collective-permute-start | bytes 1032200 | tf_op jit(solution)/shard_map/ppermute | solution.py:737
  18.2 15.9 %collective-permute-start.11 = (bf16[4,112,384]{2,1,0:T(8,128)(2,1)S(1)}, bf16[4,112,384]{2,1,0:T(8,128)(2,1)S(1)}, u32[]{:S(2)}, u32[]{:S(2)}) collective-permute-start(bf16[4,112,384]{2,1,0:T(8,128)(2,1)S(1)} %constant_dynamic-update-slice_fusion.refs_0_), channel_id=1, source_target_pairs={{0,4},{1,5},{2,6},{3,7},{4,0},{5,1},{6,2},{7,3},{8,12},{9,13},{10,... | collective-permute-start | bytes 1032200 | tf_op jit(solution)/shard_map/ppermute | solution.py:737
  18.7 15.6 %collective-permute-start.10 = (bf16[4,112,384]{2,1,0:T(8,128)(2,1)S(1)}, bf16[4,112,384]{2,1,0:T(8,128)(2,1)S(1)}, u32[]{:S(2)}, u32[]{:S(2)}) collective-permute-start(bf16[4,112,384]{2,1,0:T(8,128)(2,1)S(1)} %constant_dynamic-update-slice_fusion.refs_0_), channel_id=1, source_target_pairs={{0,2},{1,3},{2,0},{3,1},{4,6},{5,7},{6,4},{7,5},{8,10},{9,11},{10,... | collective-permute-start | bytes 1032200 | tf_op jit(solution)/shard_map/ppermute | solution.py:737
  19.3 13.9 %collective-permute-start.8 = (bf16[1,112,384]{2,1,0:T(8,128)(2,1)S(1)}, bf16[1,112,384]{2,1,0:T(8,128)(2,1)S(1)}, u32[]{:S(2)}, u32[]{:S(2)}) collective-permute-start(bf16[1,112,384]{2,1,0:T(8,128)(2,1)S(1)} %fusion.8), channel_id=1, source_target_pairs={{0,24},{1,25},{2,26},{3,27},{4,28},{5,29},{6,30},{7,31},{8,16},{9,... | collective-permute-start | bytes 258056 | tf_op jit(solution)/shard_map/ppermute | solution.py:737
  22.0 4.9 %collective-permute-start.6 = (bf16[1,112,384]{2,1,0:T(8,128)(2,1)S(1)}, bf16[1,112,384]{2,1,0:T(8,128)(2,1)S(1)}, u32[]{:S(2)}, u32[]{:S(2)}) collective-permute-start(bf16[1,112,384]{2,1,0:T(8,128)(2,1)S(1)} %fusion.8), channel_id=1, source_target_pairs={{0,8},{1,9},{2,10},{3,11},{4,12},{5,13},{6,14},{7,15},{8,0},{9,1},... | collective-permute-start | bytes 258056 | tf_op jit(solution)/shard_map/ppermute | solution.py:737
  26.9 6.3 %collective-permute-start.7 = (bf16[1,112,384]{2,1,0:T(8,128)(2,1)S(1)}, bf16[1,112,384]{2,1,0:T(8,128)(2,1)S(1)}, u32[]{:S(2)}, u32[]{:S(2)}) collective-permute-start(bf16[1,112,384]{2,1,0:T(8,128)(2,1)S(1)} %fusion.8), channel_id=1, source_target_pairs={{0,16},{1,17},{2,18},{3,19},{4,20},{5,21},{6,22},{7,23},{8,24},{9,... | collective-permute-start | bytes 258056 | tf_op jit(solution)/shard_map/ppermute | solution.py:737
  33.3 4.3 %collective-permute-start.13 = (bf16[4,112,384]{2,1,0:T(8,128)(2,1)S(1)}, bf16[4,112,384]{2,1,0:T(8,128)(2,1)S(1)}, u32[]{:S(2)}, u32[]{:S(2)}) collective-permute-start(bf16[4,112,384]{2,1,0:T(8,128)(2,1)S(1)} %constant_dynamic-update-slice_fusion.refs_0_), channel_id=1, source_target_pairs={{0,1},{1,0},{2,3},{3,2},{4,5},{5,4},{6,7},{7,6},{8,9},{9,8},{10,11... | collective-permute-start | bytes 1032200 | tf_op jit(solution)/shard_map/ppermute | solution.py:737
  33.8 4.5 %collective-permute-start.16 = (bf16[4,112,384]{2,1,0:T(8,128)(2,1)S(1)}, bf16[4,112,384]{2,1,0:T(8,128)(2,1)S(1)}, u32[]{:S(2)}, u32[]{:S(2)}) collective-permute-start(bf16[4,112,384]{2,1,0:T(8,128)(2,1)S(1)} %collective-permute-done.12.refs_3_), channel_id=1, source_target_pairs={{0,1},{1,0},{2,3},{3,2},{4,5},{5,4},{6,7},{7,6},{8,9},{9,8},{10,11... | collective-permute-start | bytes 1032200 | tf_op jit(solution)/shard_map/ppermute | solution.py:737
  34.1 4.9 %collective-permute-start.15 = (bf16[4,112,384]{2,1,0:T(8,128)(2,1)S(1)}, bf16[4,112,384]{2,1,0:T(8,128)(2,1)S(1)}, u32[]{:S(2)}, u32[]{:S(2)}) collective-permute-start(bf16[4,112,384]{2,1,0:T(8,128)(2,1)S(1)} %collective-permute-done.11.refs_2_), channel_id=1, source_target_pairs={{0,1},{1,0},{2,3},{3,2},{4,5},{5,4},{6,7},{7,6},{8,9},{9,8},{10,11... | collective-permute-start | bytes 1032200 | tf_op jit(solution)/shard_map/ppermute | solution.py:737
  34.3 4.6 %collective-permute-start.14 = (bf16[4,112,384]{2,1,0:T(8,128)(2,1)S(1)}, bf16[4,112,384]{2,1,0:T(8,128)(2,1)S(1)}, u32[]{:S(2)}, u32[]{:S(2)}) collective-permute-start(bf16[4,112,384]{2,1,0:T(8,128)(2,1)S(1)} %collective-permute-done.10.refs_1_), channel_id=1, source_target_pairs={{0,1},{1,0},{2,3},{3,2},{4,5},{5,4},{6,7},{7,6},{8,9},{9,8},{10,11... | collective-permute-start | bytes 1032200 | tf_op jit(solution)/shard_map/ppermute | solution.py:737
  35.3 39.7 %collective-permute-start.19 = (bf16[2,4,112,384]{3,2,1,0:T(8,128)(2,1)S(1)}, bf16[2,4,112,384]{3,2,1,0:T(8,128)(2,1)}, u32[]{:S(2)}, u32[]{:S(2)}) collective-permute-start(bf16[2,4,112,384]{3,2,1,0:T(8,128)(2,1)S(1)} %pad_maximum_fusion.refs_0_), channel_id=1, source_target_pairs={{0,6},{1,7},{2,4},{3,5},{4,2},{5,3},{6,0},{7,1},{8,14},{9,15},{10,... | collective-permute-start | bytes 2064392 | tf_op jit(solution)/shard_map/ppermute | solution.py:737
  37.6 37.3 %collective-permute-start.18 = (bf16[2,4,112,384]{3,2,1,0:T(8,128)(2,1)S(1)}, bf16[2,4,112,384]{3,2,1,0:T(8,128)(2,1)}, u32[]{:S(2)}, u32[]{:S(2)}) collective-permute-start(bf16[2,4,112,384]{3,2,1,0:T(8,128)(2,1)S(1)} %pad_maximum_fusion.refs_0_), channel_id=1, source_target_pairs={{0,4},{1,5},{2,6},{3,7},{4,0},{5,1},{6,2},{7,3},{8,12},{9,13},{10,... | collective-permute-start | bytes 2064392 | tf_op jit(solution)/shard_map/ppermute | solution.py:737
  38.3 36.6 %collective-permute-start.17 = (bf16[2,4,112,384]{3,2,1,0:T(8,128)(2,1)S(1)}, bf16[2,4,112,384]{3,2,1,0:T(8,128)(2,1)}, u32[]{:S(2)}, u32[]{:S(2)}) collective-permute-start(bf16[2,4,112,384]{3,2,1,0:T(8,128)(2,1)S(1)} %pad_maximum_fusion.refs_0_), channel_id=1, source_target_pairs={{0,2},{1,3},{2,0},{3,1},{4,6},{5,7},{6,4},{7,5},{8,10},{9,11},{10,... | collective-permute-start | bytes 2064392 | tf_op jit(solution)/shard_map/ppermute | solution.py:737
  126.8 79.8 %collective-permute-start.20 = (bf16[1,1024,384]{2,1,0:T(8,128)(2,1)}, bf16[1,1024,384]{2,1,0:T(8,128)(2,1)S(1)}, u32[]{:S(2)}, u32[]{:S(2)}) collective-permute-start(bf16[1,1024,384]{2,1,0:T(8,128)(2,1)} %get-tuple-element.109), channel_id=1, source_target_pairs={{0,1},{1,0},{2,3},{3,2},{4,5},{5,4},{6,7},{7,6},{8,9},{9,8},{10,11... | collective-permute-start | bytes 2359304 | tf_op jit(solution)/shard_map/ppermute | solution.py:737
  132.5 71.8 %collective-permute-start.22 = (bf16[464,384]{1,0:T(8,128)(2,1)}, bf16[464,384]{1,0:T(8,128)(2,1)}, u32[]{:S(2)}, u32[]{:S(2)}) collective-permute-start(bf16[464,384]{1,0:T(8,128)(2,1)} %get-tuple-element.116), channel_id=1, source_target_pairs={{0,2},{1,3},{2,0},{3,1},{4,6},{5,7},{6,4},{7,5},{8,10},{9,11},{10,... | collective-permute-start | bytes 1069064 | tf_op jit(solution)/shard_map/ppermute | solution.py:737
  158.3 46.0 %collective-permute-start.23 = (bf16[464,384]{1,0:T(8,128)(2,1)}, bf16[464,384]{1,0:T(8,128)(2,1)}, u32[]{:S(2)}, u32[]{:S(2)}) collective-permute-start(bf16[464,384]{1,0:T(8,128)(2,1)} %get-tuple-element.117), channel_id=1, source_target_pairs={{0,4},{1,5},{2,6},{3,7},{4,0},{5,1},{6,2},{7,3},{8,12},{9,13},{10,... | collective-permute-start | bytes 1069064 | tf_op jit(solution)/shard_map/ppermute | solution.py:737
  182.2 22.1 %collective-permute-start.24 = (bf16[464,384]{1,0:T(8,128)(2,1)}, bf16[464,384]{1,0:T(8,128)(2,1)}, u32[]{:S(2)}, u32[]{:S(2)}) collective-permute-start(bf16[464,384]{1,0:T(8,128)(2,1)} %get-tuple-element.118), channel_id=1, source_target_pairs={{0,6},{1,7},{2,4},{3,5},{4,2},{5,3},{6,0},{7,1},{8,14},{9,15},{10,... | collective-permute-start | bytes 1069064 | tf_op jit(solution)/shard_map/ppermute | solution.py:737
  229.7 4.5 %collective-permute-start.26 = (bf16[16,40,384]{2,1,0:T(8,128)(2,1)}, bf16[16,40,384]{2,1,0:T(8,128)(2,1)S(1)}, u32[]{:S(2)}, u32[]{:S(2)}) collective-permute-start(bf16[16,40,384]{2,1,0:T(8,128)(2,1)} %get-tuple-element.134), channel_id=1, source_target_pairs={{0,1},{1,0},{2,3},{3,2},{4,5},{5,4},{6,7},{7,6},{8,9},{9,8},{10,11... | collective-permute-start | bytes 1474568 | tf_op jit(solution)/shard_map/ppermute | solution.py:737
  229.8 7.5 %collective-permute-start.33 = (bf16[176,384]{1,0:T(8,128)(2,1)}, bf16[176,384]{1,0:T(8,128)(2,1)S(1)}, u32[]{:S(2)}, u32[]{:S(2)}) collective-permute-start(bf16[176,384]{1,0:T(8,128)(2,1)} %get-tuple-element.145), channel_id=1, source_target_pairs={{0,8},{1,9},{2,10},{3,11},{4,12},{5,13},{6,14},{7,15},{8,0},{9,1},... | collective-permute-start | bytes 405512 | tf_op jit(solution)/shard_map/ppermute | solution.py:737
  229.8 37.5 %collective-permute-start.34 = (bf16[176,384]{1,0:T(8,128)(2,1)}, bf16[176,384]{1,0:T(8,128)(2,1)S(1)}, u32[]{:S(2)}, u32[]{:S(2)}) collective-permute-start(bf16[176,384]{1,0:T(8,128)(2,1)} %get-tuple-element.146), channel_id=1, source_target_pairs={{0,16},{1,17},{2,18},{3,19},{4,20},{5,21},{6,22},{7,23},{8,24},{9,... | collective-permute-start | bytes 405512 | tf_op jit(solution)/shard_map/ppermute | solution.py:737
  229.9 37.5 %collective-permute-start.35 = (bf16[176,384]{1,0:T(8,128)(2,1)S(1)}, bf16[176,384]{1,0:T(8,128)(2,1)S(1)}, u32[]{:S(2)}, u32[]{:S(2)}) collective-permute-start(bf16[176,384]{1,0:T(8,128)(2,1)S(1)} %copy-done.25), channel_id=1, source_target_pairs={{0,24},{1,25},{2,26},{3,27},{4,28},{5,29},{6,30},{7,31},{8,16},{9,... | collective-permute-start | bytes 405512 | tf_op jit(solution)/shard_map/ppermute | solution.py:737
  234.2 39.8 %collective-permute-start.25 = (bf16[1,1024,384]{2,1,0:T(8,128)(2,1)}, bf16[1,1024,384]{2,1,0:T(8,128)(2,1)S(1)}, u32[]{:S(2)}, u32[]{:S(2)}) collective-permute-start(bf16[1,1024,384]{2,1,0:T(8,128)(2,1)} %get-tuple-element.130), channel_id=1, source_target_pairs={{0,1},{1,0},{2,3},{3,2},{4,5},{5,4},{6,7},{7,6},{8,9},{9,8},{10,11... | collective-permute-start | bytes 2359304 | tf_op jit(solution)/shard_map/ppermute | solution.py:737
  235.7 34.3 %collective-permute-start.29 = (bf16[168,384]{1,0:T(8,128)(2,1)S(1)}, bf16[168,384]{1,0:T(8,128)(2,1)S(1)}, u32[]{:S(2)}, u32[]{:S(2)}) collective-permute-start(bf16[168,384]{1,0:T(8,128)(2,1)S(1)} %get-tuple-element.176), channel_id=1, source_target_pairs={{0,6},{1,7},{2,4},{3,5},{4,2},{5,3},{6,0},{7,1},{8,14},{9,15},{10,... | collective-permute-start | bytes 387080 | tf_op jit(solution)/shard_map/ppermute | solution.py:737
  237.2 35.5 %collective-permute-start.28 = (bf16[168,384]{1,0:T(8,128)(2,1)S(1)}, bf16[168,384]{1,0:T(8,128)(2,1)S(1)}, u32[]{:S(2)}, u32[]{:S(2)}) collective-permute-start(bf16[168,384]{1,0:T(8,128)(2,1)S(1)} %get-tuple-element.177), channel_id=1, source_target_pairs={{0,4},{1,5},{2,6},{3,7},{4,0},{5,1},{6,2},{7,3},{8,12},{9,13},{10,... | collective-permute-start | bytes 387080 | tf_op jit(solution)/shard_map/ppermute | solution.py:737
  267.4 6.6 %collective-permute-start.27 = (bf16[168,384]{1,0:T(8,128)(2,1)S(1)}, bf16[168,384]{1,0:T(8,128)(2,1)S(1)}, u32[]{:S(2)}, u32[]{:S(2)}) collective-permute-start(bf16[168,384]{1,0:T(8,128)(2,1)S(1)} %get-tuple-element.178), channel_id=1, source_target_pairs={{0,2},{1,3},{2,0},{3,1},{4,6},{5,7},{6,4},{7,5},{8,10},{9,11},{10,... | collective-permute-start | bytes 387080 | tf_op jit(solution)/shard_map/ppermute | solution.py:737
  270.0 13.8 %collective-permute-start.37 = (bf16[256,384]{1,0:T(8,128)(2,1)}, bf16[256,384]{1,0:T(8,128)(2,1)S(1)}, u32[]{:S(2)}, u32[]{:S(2)}) collective-permute-start(bf16[256,384]{1,0:T(8,128)(2,1)} %get-tuple-element.152.mine2), channel_id=1, source_target_pairs={{0,1},{1,0},{2,3},{3,2},{4,5},{5,4},{6,7},{7,6},{8,9},{9,8},{10,11... | collective-permute-start | bytes 589832 | tf_op jit(solution)/shard_map/ppermute | solution.py:737
  275.1 6.6 %collective-permute-start.32 = (bf16[72,384]{1,0:T(8,128)(2,1)S(1)}, bf16[72,384]{1,0:T(8,128)(2,1)S(1)}, u32[]{:S(2)}, u32[]{:S(2)}) collective-permute-start(bf16[72,384]{1,0:T(8,128)(2,1)S(1)} %get-tuple-element.173), channel_id=1, source_target_pairs={{0,24},{1,25},{2,26},{3,27},{4,28},{5,29},{6,30},{7,31},{8,16},{9,... | collective-permute-start | bytes 165896 | tf_op jit(solution)/shard_map/ppermute | solution.py:737
  275.1 6.5 %collective-permute-start.31 = (bf16[72,384]{1,0:T(8,128)(2,1)S(1)}, bf16[72,384]{1,0:T(8,128)(2,1)S(1)}, u32[]{:S(2)}, u32[]{:S(2)}) collective-permute-start(bf16[72,384]{1,0:T(8,128)(2,1)S(1)} %get-tuple-element.174), channel_id=1, source_target_pairs={{0,16},{1,17},{2,18},{3,19},{4,20},{5,21},{6,22},{7,23},{8,24},{9,... | collective-permute-start | bytes 165896 | tf_op jit(solution)/shard_map/ppermute | solution.py:737
  275.8 6.4 %collective-permute-start.30 = (bf16[72,384]{1,0:T(8,128)(2,1)S(1)}, bf16[72,384]{1,0:T(8,128)(2,1)S(1)}, u32[]{:S(2)}, u32[]{:S(2)}) collective-permute-start(bf16[72,384]{1,0:T(8,128)(2,1)S(1)} %get-tuple-element.175), channel_id=1, source_target_pairs={{0,8},{1,9},{2,10},{3,11},{4,12},{5,13},{6,14},{7,15},{8,0},{9,1},... | collective-permute-start | bytes 165896 | tf_op jit(solution)/shard_map/ppermute | solution.py:737
  (32 other events, 287.9 us)
